TPU v7x, 512 devices: a whole 4x8x8 slice. The times are simulated.
512 devices in a mesh: dp: 16 (over z_lo, y), seq: 32 (over z_hi, x, core).
Axes of the slice: x: 4, y: 8, z: 8 (z_hi: 4, z_lo: 2; z = z_hi * 2 + z_lo), core: 2. Of those that a mesh axis runs over, the one named last changes fastest.
Arguments:
- latents: bfloat16 [512, 16, 16384], P('dp', None, 'seq'), may hold values from -8 to 8, as said below
- noise: bfloat16 [512, 16, 16384], P('dp', None, 'seq'), may hold values from -6 to 6
Outputs:
- targets: bfloat16 [512, 16, 16384], P('dp', None, 'seq')
- row_potential: float32 [512], replicated
- column_potential: float32 [512], P('dp')
Inputs may be any that keep to these rules, and one draw needn't show every extreme that they name: `latents`: each clip's values have a clip-dependent scale.
All inputs are finite; a program needn't handle non-finite values.
Results may differ from a plain program's by a relative error of at most 0.0065.
Values may be sent and summed in bfloat16 or wider, within the bound.
No kernel may reach another device: no remote copies, remote signals or barrier semaphores. Data moves between devices by JAX's collectives and lax.ppermute only.
A program may use at most 64 MiB of HBM per device.

v0:
```python
import math

import jax
import jax.numpy as jnp
from jax import lax
from jax.sharding import PartitionSpec as P

ITERS = 4


blur = 0.5


def pair_block(piece, flat_latents, latent_norms):
    flat_piece = piece.reshape(piece.shape[0], -1)
    cross = lax.dot_general(
        flat_piece, flat_latents, (((1,), (1,)), ((), ())), preferred_element_type=jnp.float32
    )
    piece_norms = jnp.einsum("kc,kc->k", flat_piece, flat_piece, preferred_element_type=jnp.float32)
    return piece_norms[:, None] + latent_norms[None, :] - 2.0 * cross


def weighted_block(weights, piece):
    flat_piece = piece.reshape(piece.shape[0], -1)
    return lax.dot_general(
        weights, flat_piece, (((0,), (0,)), ((), ())), preferred_element_type=jnp.float32
    )


def per_device(latents, noise):
    local_clips, channels, positions = latents.shape
    total_clips = local_clips * lax.axis_size("dp")
    scale = math.sqrt(channels * positions * lax.axis_size("seq"))
    log_mass = -math.log(total_clips)
    flat_latents = latents.reshape(local_clips, channels * positions)
    latent_norms = jnp.einsum(
        "kc,kc->k", flat_latents, flat_latents, preferred_element_type=jnp.float32
    )
    gathered = lax.all_gather(noise, "dp", axis=0, tiled=True)
    partial_value = pair_block(gathered, flat_latents, latent_norms)
    summed = lax.psum(partial_value, "seq")
    cost = summed / scale
    row_potential = jnp.zeros((total_clips,), jnp.float32)
    column_potential = jnp.zeros((local_clips,), jnp.float32)
    for step in range(ITERS):
        column_scores = (row_potential[:, None] - cost) / blur
        column_top = jnp.max(column_scores, axis=0)
        column_total = jnp.sum(jnp.exp(column_scores - column_top[None, :]), axis=0)
        column_potential = blur * log_mass - blur * (column_top + jnp.log(column_total))
        row_scores = (column_potential[None, :] - cost) / blur
        row_top = lax.pmax(jnp.max(row_scores, axis=1), "dp")
        row_total = lax.psum(jnp.sum(jnp.exp(row_scores - row_top[:, None]), axis=1), "dp")
        row_potential = blur * log_mass - blur * (row_top + jnp.log(row_total))
    plan = jnp.exp((row_potential[:, None] + column_potential[None, :] - cost) / blur)
    weights = (plan / jnp.sum(plan, axis=0)[None, :]).astype(jnp.bfloat16)
    moved = weighted_block(weights, gathered)
    targets = moved.astype(jnp.bfloat16).reshape(local_clips, channels, positions)
    return (targets, row_potential, column_potential)


def solution(mesh):
    in_specs = (P("dp", None, "seq"), P("dp", None, "seq"))
    out_specs = (P("dp", None, "seq"), P(), P("dp"))
    return jax.shard_map(
        per_device, mesh=mesh, in_specs=in_specs, out_specs=out_specs, check_vma=False
    )
```

profile of v0, /device:TPU:8, one launch (start us, length us, event | category | flops | bytes accessed | tf_op | source)
XLA Modules:
  0.0 681.6 jit_solution(5769714332488169832)
XLA Ops:
  7.2 0.0 all-gather.2.cloned.1.call-start
  7.2 2.1 copy.7
  9.3 0.0 all-gather.2.cloned.1.call-update
  9.4 0.0 all-reduce.2.cloned.1.call-start
  9.4 1.3 copy.19
  10.8 0.2 fusion.3
  11.0 105.5 %all-gather.2.cloned.1.call-done = bf16[512,16,512]{2,0,1:T(8,128)(2,1)} async-done(((bf16[32,16,512]{2,0,1:T(8,128)(2,1)}), bf16[512,16,512]{2,0,1:T(8,128)(2,1)}) %all-gather.2.cloned.1.call-update) | async-done | bytes 8388624 | tf_op jit(solution)/shard_map/all_gather | solution.py:39
  116.5 0.0 copy-start.1
  116.5 12.4 %copy.18 = bf16[512,16,512]{0,2,1:T(8,128)(2,1)} copy(bf16[512,16,512]{2,0,1:T(8,128)(2,1)} %all-gather.2.cloned.1.call-done) | data formatting | bytes 16777216 | tf_op jit(solution)/shard_map/reshape | solution.py:15
  128.8 0.0 copy-start
  128.8 5.3 fusion
  134.1 0.0 copy-done.1
  134.2 0.5 copy-done
  134.6 3.2 fusion.2
  137.8 0.0 all-reduce.2.cloned.1.call-update
  137.8 257.9 %all-reduce.2.cloned.1.call-done = f32[512,32]{0,1:T(8,128)} async-done(((f32[512,32]{0,1:T(8,128)}), f32[512,32]{0,1:T(8,128)}) %all-reduce.2.cloned.1.call-update) | async-done | bytes 65552 | tf_op jit(solution)/shard_map/psum | solution.py:41
  395.8 1.0 fusion.5
  396.7 1.0 exponential_reduce_fusion.7
  397.8 0.9 fusion.6
  398.7 32.4 %pmax.28 = f32[512]{0:T(512)S(1)} all-reduce(f32[512]{0:T(512)S(1)} %fusion.6), channel_id=1, replica_groups=mesh['dp'=16,'seq'=32] {'dp'}, use_global_device_ids=true, to_apply=%region_4.0 | all-reduce | flops 512 | bytes 4096 | tf_op jit(solution)/shard_map/pmax | solution.py:51
  431.1 0.9 exponential_reduce_fusion.6
  432.0 33.3 %psum.36 = f32[512]{0:T(512)S(1)} all-reduce(f32[512]{0:T(512)S(1)} %exponential_reduce_fusion.6), channel_id=1, replica_groups=mesh['dp'=16,'seq'=32] {'dp'}, use_global_device_ids=true, to_apply=%region_6.0 | all-reduce | flops 512 | bytes 4096 | tf_op jit(solution)/shard_map/psum | solution.py:52
  465.3 1.0 fusion.7
  466.3 1.0 exponential_reduce_fusion.5
  467.3 0.9 fusion.8
  468.3 30.6 %pmax.29 = f32[512]{0:T(512)S(1)} all-reduce(f32[512]{0:T(512)S(1)} %fusion.8), channel_id=1, replica_groups=mesh['dp'=16,'seq'=32] {'dp'}, use_global_device_ids=true, to_apply=%region_10.0 | all-reduce | flops 512 | bytes 4096 | tf_op jit(solution)/shard_map/pmax | solution.py:51
  498.9 0.9 exponential_reduce_fusion.4
  499.8 32.6 %psum.37 = f32[512]{0:T(512)S(1)} all-reduce(f32[512]{0:T(512)S(1)} %exponential_reduce_fusion.4), channel_id=1, replica_groups=mesh['dp'=16,'seq'=32] {'dp'}, use_global_device_ids=true, to_apply=%region_12.0 | all-reduce | flops 512 | bytes 4096 | tf_op jit(solution)/shard_map/psum | solution.py:52
  532.5 1.0 fusion.9
  533.4 1.0 exponential_reduce_fusion.3
  534.5 0.9 fusion.10
  535.4 30.6 %pmax.30 = f32[512]{0:T(512)S(1)} all-reduce(f32[512]{0:T(512)S(1)} %fusion.10), channel_id=1, replica_groups=mesh['dp'=16,'seq'=32] {'dp'}, use_global_device_ids=true, to_apply=%region_16.0 | all-reduce | flops 512 | bytes 4096 | tf_op jit(solution)/shard_map/pmax | solution.py:51
  566.0 0.9 exponential_reduce_fusion.2
  567.0 32.6 %psum.38 = f32[512]{0:T(512)S(1)} all-reduce(f32[512]{0:T(512)S(1)} %exponential_reduce_fusion.2), channel_id=1, replica_groups=mesh['dp'=16,'seq'=32] {'dp'}, use_global_device_ids=true, to_apply=%region_18.0 | all-reduce | flops 512 | bytes 4096 | tf_op jit(solution)/shard_map/psum | solution.py:52
  599.6 1.0 fusion.11
  600.6 1.0 exponential_reduce_fusion.1
  601.6 0.0 copy-start.3
  601.6 0.9 fusion.12
  602.6 30.6 %pmax.31 = f32[512]{0:T(512)S(1)} all-reduce(f32[512]{0:T(512)S(1)} %fusion.12), channel_id=1, replica_groups=mesh['dp'=16,'seq'=32] {'dp'}, use_global_device_ids=true, to_apply=%region_22.0 | all-reduce | flops 512 | bytes 4096 | tf_op jit(solution)/shard_map/pmax | solution.py:51
  633.2 0.9 exponential_reduce_fusion
  634.1 32.6 %psum.39 = f32[512]{0:T(512)S(1)} all-reduce(f32[512]{0:T(512)S(1)} %exponential_reduce_fusion), channel_id=1, replica_groups=mesh['dp'=16,'seq'=32] {'dp'}, use_global_device_ids=true, to_apply=%region_24.0 | all-reduce | flops 512 | bytes 4096 | tf_op jit(solution)/shard_map/psum | solution.py:52
  666.7 0.0 copy-start.2
  666.7 1.0 fusion.13
  667.8 6.0 convolution_convert_fusion
  673.8 1.0 copy.20
  674.7 0.0 copy-done.3
  674.7 0.0 copy-done.2
  (8 shorter events, 0.1 us)
Async XLA Ops:
  7.2 109.3 %all-gather.2.cloned.1.call-start = ((), (), s32[]{:S(2)}) async-start(), calls=%async_computation | async-start | bytes 8912896 | tf_op jit(solution)/shard_map/all_gather | solution.py:39
  9.4 386.4 %all-reduce.2.cloned.1.call-start = ((), (), s32[]{:S(2)}) async-start(), calls=%async_computation.1 | async-start | bytes 131072 | tf_op jit(solution)/shard_map/psum | solution.py:41
  116.5 17.7 %copy-start.1 = (bf16[32,16,512]{2,1,0:T(8,128)(2,1)S(1)}, bf16[32,16,512]{2,1,0:T(8,128)(2,1)}, u32[]{:S(2)}) copy-start(bf16[32,16,512]{2,1,0:T(8,128)(2,1)} %param.2) | copy-start | bytes 1572868
  128.8 5.8 copy-start
  601.6 73.1 %copy-start.3 = (f32[32]{0:T(128)}, f32[32]{0:T(128)S(1)}, u32[]{:S(2)}) copy-start(f32[32]{0:T(128)S(1)} %multiply_subtract_fusion.4) | copy-start | bytes 388
  666.7 8.0 %copy-start.2 = (f32[512]{0:T(512)}, f32[512]{0:T(512)S(1)}, u32[]{:S(2)}) copy-start(f32[512]{0:T(512)S(1)} %multiply_subtract_fusion) | copy-start | bytes 6148
Sparse Core Ops, SparseCore 0:
  10.7 105.7 all-gather.1
  138.0 257.7 all-reduce.1
where the time goes:
time: 683 us; the launch traced here: 682 us
  waiting for transfers between devices  363 us (53%)
  blocking collectives  255 us (37%)
  other arithmetic  22.2 us (3%)
  local copies, waits for them, and re-layouts  17.2 us (3%)
  between operations  14.1 us (2%)
  matrix products  9.17 us (1%)
    psum x1, waiting for transfers between devices, per_device(): summed = lax.psum(partial_value, 'seq')  258 us
    psum x4, blocking collectives, per_device(): lax.psum(jnp.sum(jnp.exp(row_scores - row_top[:, None]), axis=1), 'dp')  131 us
    pmax x4, blocking collectives, per_device(): row_top = lax.pmax(jnp.max(row_scores, axis=1), 'dp')  124 us
    all_gather x1, waiting for transfers between devices, per_device(): gathered = lax.all_gather(noise, 'dp', axis=0, tiled=True)  105 us
  transfers between devices with their start and end apart: 2, of which 2 were waited for; matrix products, arithmetic and copies ran while one was open for 0% of the time, Pallas kernels for 0%

commit v1 on v0

v1 whole, which is shorter than its diff:
```python
import functools
import math

import jax
import jax.numpy as jnp
from jax import lax
from jax.experimental import pallas as pl
from jax.experimental.pallas import tpu as pltpu
from jax.sharding import PartitionSpec as P

ITERS = 4
BLUR = 0.5
CORES = 2
VMEM = pl.BlockSpec(memory_space=pltpu.VMEM)
SMEM = pl.BlockSpec(memory_space=pltpu.SMEM)
LIMIT = pltpu.CompilerParams(vmem_limit_bytes=32 * 1024 * 1024)


def pair_kernel(core_ref, clips_ref, send_ref, keep_ref):
    sources, both, width = clips_ref.shape
    local = both // 2
    half = sources // CORES
    core = core_ref[0]
    noise = clips_ref[:, :local, :].reshape(sources * local, width)
    wide = noise.astype(jnp.float32)
    noise_norms = jnp.sum(wide * wide, axis=1, keepdims=True)
    for first, out_ref in ((half * (1 - core), send_ref), (half * core, keep_ref)):
        latents = clips_ref[pl.ds(first, half), local:, :].reshape(half * local, width)
        wide = latents.astype(jnp.float32)
        latent_norms = jnp.sum(wide * wide, axis=1, keepdims=True)
        latent_norms = jnp.transpose(jnp.broadcast_to(latent_norms, (half * local, 128)))[:1, :]
        cross = lax.dot_general(
            noise, latents, (((1,), (1,)), ((), ())), preferred_element_type=jnp.float32
        )
        out_ref[...] = noise_norms + latent_norms - 2.0 * cross


def spread_kernel(parts_ref, out_ref):
    out_ref[...] = jnp.broadcast_to(jnp.sum(parts_ref[...], axis=0)[None], out_ref.shape)


def coupling_kernel(factor, core_ref, own_ref, other_ref, clips_ref, moved_ref, row_ref, column_ref, *scores):
    sources, both, width = clips_ref.shape
    local = both // 2
    core = core_ref[0]
    total = sources * local
    log_mass = -math.log2(total)
    for score, given in zip(scores, (own_ref, other_ref), strict=True):
        score[...] = given[...] * factor
    row = jnp.zeros((total, 1), jnp.float32)
    columns = [None] * CORES
    for step in range(ITERS):
        for k, score in enumerate(scores):
            value = row - score[...]
            top = jnp.max(value, axis=0, keepdims=True)
            mass = jnp.sum(jnp.exp2(value - top), axis=0, keepdims=True)
            columns[k] = log_mass - (top + jnp.log2(mass))
        values = [column - score[...] for column, score in zip(columns, scores, strict=True)]
        top = jnp.max(jnp.maximum(*values), axis=1, keepdims=True)
        mass = jnp.sum(sum(jnp.exp2(value - top) for value in values), axis=1, keepdims=True)
        row = log_mass - (top + jnp.log2(mass))
    noise = clips_ref[:, :local, :].reshape(total, width)
    back = BLUR * math.log(2.0)
    row_ref[...] = jnp.transpose(jnp.broadcast_to(row * back, (total, 128)))[:8, :]
    for k, (column, score) in enumerate(zip(columns, scores, strict=True)):
        place = core if k == 0 else 1 - core
        plan = jnp.exp2((row + column) - score[...])
        weights = (plan / jnp.sum(plan, axis=0, keepdims=True)).astype(jnp.bfloat16)
        moved = lax.dot_general(
            weights, noise, (((0,), (0,)), ((), ())), preferred_element_type=jnp.float32
        )
        moved_ref[place] = moved.astype(jnp.bfloat16)
        column_ref[place] = jnp.broadcast_to(column * back, column_ref.shape[1:])


def per_device(latents, noise):
    local, channels, width = latents.shape
    dp, seq = lax.axis_size("dp"), lax.axis_size("seq")
    total = local * dp
    half = total // CORES
    factor = math.log2(math.e) / (BLUR * math.sqrt(channels * width * seq))
    core = lax.rem(lax.axis_index("seq"), CORES)
    core_scalar = core.reshape(1).astype(jnp.int32)
    swap = [(i, i ^ 1) for i in range(seq)]
    chips = [list(range(c, seq, CORES)) for c in range(CORES)]

    packed = jnp.concatenate([noise, latents], axis=0).swapaxes(0, 1)
    clips = lax.all_to_all(packed, "dp", 0, 0, tiled=True)

    block = jax.ShapeDtypeStruct((total, half), jnp.float32)
    send, keep = pl.pallas_call(
        pair_kernel,
        out_shape=(block, block),
        in_specs=[SMEM, VMEM],
        out_specs=(VMEM, VMEM),
        compiler_params=LIMIT,
    )(core_scalar, clips)
    summed = keep + lax.ppermute(send, "seq", swap)

    spread = pl.pallas_call(
        spread_kernel,
        out_shape=jax.ShapeDtypeStruct((dp, local, half), jnp.float32),
        in_specs=[VMEM],
        out_specs=VMEM,
        compiler_params=LIMIT,
    )
    parts = lax.all_to_all(summed.reshape(dp, local, half), "dp", 0, 0, tiled=True)
    parts = lax.all_to_all(spread(parts), "seq", 0, 0, tiled=True, axis_index_groups=chips)
    own = lax.all_to_all(spread(parts), "dp", 0, 0, tiled=True).reshape(total, half)
    other = lax.ppermute(own, "seq", swap)

    moved, row, column = pl.pallas_call(
        functools.partial(coupling_kernel, factor),
        out_shape=(
            jax.ShapeDtypeStruct((CORES, half, width), jnp.bfloat16),
            jax.ShapeDtypeStruct((8, total), jnp.float32),
            jax.ShapeDtypeStruct((CORES, 8, half), jnp.float32),
        ),
        in_specs=[SMEM, VMEM, VMEM, VMEM],
        out_specs=(VMEM, VMEM, VMEM),
        scratch_shapes=[pltpu.VMEM((total, half), jnp.float32)] * CORES,
        compiler_params=LIMIT,
    )(core_scalar, own, other, clips)
    back = lax.all_to_all(moved.reshape(dp, local, width), "dp", 0, 0, tiled=True)
    targets = back.swapaxes(0, 1)
    column = lax.dynamic_slice(
        column[:, 0, :].reshape(total), (lax.axis_index("dp") * local,), (local,)
    )
    return (targets, row[0], column)


def solution(mesh):
    in_specs = (P("dp", None, "seq"), P("dp", None, "seq"))
    out_specs = (P("dp", None, "seq"), P(), P("dp"))
    return jax.shard_map(
        per_device, mesh=mesh, in_specs=in_specs, out_specs=out_specs, check_vma=False
    )
```

time: 683 us -> 144 us (0.21)
  waiting for transfers between devices: 363 us -> 44.5 us
  blocking collectives: 255 us -> 70.3 us
  other arithmetic: 22.2 us -> 1.1 us
  starting transfers between devices: 0.08 us -> 18.5 us
  between operations: 14.1 us -> 0.7 us
  local copies, waits for them, and re-layouts: 17.2 us -> 3.94 us
  matrix products: 9.17 us -> 0 us
    psum x1 -> x0, waiting for transfers between devices: 258 us -> none  [per_device(): summed = lax.psum(partial_value, 'seq')]
    psum x4 -> x0, blocking collectives: 131 us -> none  [per_device(): lax.psum(jnp.sum(jnp.exp(row_scores - row_top[:, None]), axis=1), 'dp')]
    pmax x4 -> x0, blocking collectives: 124 us -> none  [per_device(): row_top = lax.pmax(jnp.max(row_scores, axis=1), 'dp')]
    all_gather x1 -> x0, waiting for transfers between devices: 105 us -> none  [per_device(): gathered = lax.all_gather(noise, 'dp', axis=0, tiled=True)]
    all_to_all x0 -> x3, blocking collectives: none -> 70.3 us  [the longest x1 25.9 us: per_device(): lax.all_to_all(spread(parts), 'seq', 0, 0, tiled=True, axis_index_groups=...]
    all_to_all x0 -> x2, waiting for transfers between devices: none -> 40.7 us  [the longest x1 26.3 us: per_device(): clips = lax.all_to_all(packed, 'dp', 0, 0, tiled=True)]
    all_to_all x0 -> x2, starting transfers between devices: none -> 14.6 us  [the longest x1 9.37 us: per_device(): clips = lax.all_to_all(packed, 'dp', 0, 0, tiled=True)]
    reshape x1 -> x0, local copies, waits for them, and re-layouts: 12.4 us -> none  [pair_block(): flat_piece = piece.reshape(piece.shape[0], -1)]
  transfers between devices with their start and end apart: 2 -> 4, of which waited for: 2 -> 4; matrix products, arithmetic and copies ran while one was open for 0% -> 1% of each run, Pallas kernels for 0% -> 0%
where the time goes in v1:
time: 144 us; the launch traced here: 143 us
  blocking collectives  70.3 us (49%)
  waiting for transfers between devices  44.5 us (31%)
  starting transfers between devices  18.5 us (13%)
  Pallas kernels  4.21 us (3%)
  local copies, waits for them, and re-layouts  3.94 us (3%)
    all_to_all x1, waiting for transfers between devices, per_device(): clips = lax.all_to_all(packed, 'dp', 0, 0, tiled=True)  26.3 us
    all_to_all x1, blocking collectives, per_device(): lax.all_to_all(spread(parts), 'seq', 0, 0, tiled=True, axis_index_groups=...  25.9 us
    all_to_all x1, blocking collectives, per_device(): lax.all_to_all(spread(parts), 'dp', 0, 0, tiled=True).reshape(total, half)  23.7 us
    all_to_all x1, blocking collectives, per_device(): lax.all_to_all(summed.reshape(dp, local, half), 'dp', 0, 0, tiled=True)  20.6 us
    all_to_all x1, waiting for transfers between devices, per_device(): lax.all_to_all(moved.reshape(dp, local, width), 'dp', 0, 0, tiled=True)  14.5 us
    all_to_all x1, starting transfers between devices, per_device(): clips = lax.all_to_all(packed, 'dp', 0, 0, tiled=True)  9.37 us
    all_to_all x1, starting transfers between devices, per_device(): lax.all_to_all(moved.reshape(dp, local, width), 'dp', 0, 0, tiled=True)  5.27 us
    pallas_call x1, Pallas kernels, per_device(): pl.pallas_call(functools.partial(coupling_kernel, factor), out_shape=(jax...  3.56 us
  transfers between devices with their start and end apart: 4, of which 4 were waited for; matrix products, arithmetic and copies ran while one was open for 1% of the time, Pallas kernels for 0%

profile of v1, /device:TPU:8, one launch (start us, length us, event | category | flops | bytes accessed | tf_op | source)
XLA Modules:
  0.0 143.2 jit_solution(7649286744051062984)
XLA Ops:
  0.6 0.0 copy-start
  0.6 1.4 copy.9
  2.0 0.0 copy-done
  2.0 0.3 copy.8
  2.3 1.0 maximum_bitcast_fusion
  3.4 9.4 %all-to-all-start = ((bf16[16,64,512]{2,1,0:T(8,128)(2,1)}), bf16[16,64,512]{2,1,0:T(8,128)(2,1)S(1)}, u32[]{:S(2)}, u32[]{:S(2)}) async-start(bf16[16,64,512]{2,1,0:T(8,128)(2,1)} %maximum_bitcast_fusion), calls=%async_computation | async-start | bytes 2097152 | tf_op jit(solution)/shard_map/all_to_all | solution.py:88
  12.7 26.3 %all-to-all-done.clips_ref = bf16[16,64,512]{2,1,0:T(8,128)(2,1)S(1)} async-done(((bf16[16,64,512]{2,1,0:T(8,128)(2,1)}), bf16[16,64,512]{2,1,0:T(8,128)(2,1)S(1)}, u32[]{:S(2)}, u32[]{:S(2)}) %all-to-all-start) | async-done | bytes 1048608 | tf_op jit(solution)/shard_map/all_to_all | solution.py:88
  39.0 0.5 shard_map.49
  39.6 1.9 %collective-permute-start = (f32[512,256]{1,0:T(8,128)S(1)}, f32[512,256]{1,0:T(8,128)S(1)}, u32[]{:S(2)}, u32[]{:S(2)}) collective-permute-start(f32[512,256]{1,0:T(8,128)S(1)} %get-tuple-element.9), channel_id=1, source_target_pairs={{0,1},{1,0},{2,3},{3,2},{4,5},{5,4},{6,7},{7,6},{8,9},{9,8},{10,11... | collective-permute-start | bytes 1572872 | tf_op jit(solution)/shard_map/ppermute | solution.py:98
  41.5 1.9 %collective-permute-done = f32[512,256]{1,0:T(8,128)S(1)} collective-permute-done((f32[512,256]{1,0:T(8,128)S(1)}, f32[512,256]{1,0:T(8,128)S(1)}, u32[]{:S(2)}, u32[]{:S(2)}) %collective-permute-start) | collective-permute-done | bytes 524320 | tf_op jit(solution)/shard_map/ppermute | solution.py:98
  43.4 0.1 add.6
  43.4 20.6 %all_to_all.25.parts_ref = f32[16,32,256]{2,1,0:T(8,128)S(1)} all-to-all(f32[16,32,256]{2,1,0:T(8,128)S(1)} %bitcast.11), channel_id=1, replica_groups=mesh['dp'=16,'seq'=32] {'dp'}, dimensions={0} | all-to-all | bytes 1048576 | tf_op jit(solution)/shard_map/all_to_all | solution.py:107
  64.1 0.1 shard_map.50
  64.1 25.9 %all_to_all.26.parts_ref = f32[16,32,256]{2,1,0:T(8,128)S(1)} all-to-all(f32[16,32,256]{2,1,0:T(8,128)S(1)} %shard_map.50), channel_id=1, replica_groups={{0,2,4,6,8,10,12,14,16,18,20,22,24,26,28,30},{1,3,5,7,9,11,13,15,17,19,..., dimensions={0} | all-to-all | bytes 1048576 | tf_op jit(solution)/shard_map/all_to_all | solution.py:108
  90.1 0.1 shard_map.51
  90.1 23.7 %all_to_all.27 = f32[16,32,256]{2,1,0:T(8,128)S(1)} all-to-all(f32[16,32,256]{2,1,0:T(8,128)S(1)} %shard_map.51), channel_id=1, replica_groups=mesh['dp'=16,'seq'=32] {'dp'}, dimensions={0} | all-to-all | bytes 1048576 | tf_op jit(solution)/shard_map/all_to_all | solution.py:109
  113.8 1.9 %collective-permute-start.1 = (f32[512,256]{1,0:T(8,128)S(1)}, f32[512,256]{1,0:T(8,128)S(1)}, u32[]{:S(2)}, u32[]{:S(2)}) collective-permute-start(f32[512,256]{1,0:T(8,128)S(1)} %bitcast.9), channel_id=1, source_target_pairs={{0,1},{1,0},{2,3},{3,2},{4,5},{5,4},{6,7},{7,6},{8,9},{9,8},{10,11... | collective-permute-start | bytes 1572872 | tf_op jit(solution)/shard_map/ppermute | solution.py:110
  115.8 1.9 %collective-permute-done.1.other_ref = f32[512,256]{1,0:T(8,128)S(1)} collective-permute-done((f32[512,256]{1,0:T(8,128)S(1)}, f32[512,256]{1,0:T(8,128)S(1)}, u32[]{:S(2)}, u32[]{:S(2)}) %collective-permute-start.1) | collective-permute-done | bytes 524320 | tf_op jit(solution)/shard_map/ppermute | solution.py:110
  117.6 3.6 %shard_map.52 = (bf16[2,256,512]{2,1,0:T(8,128)(2,1)}, f32[8,512]{1,0:T(8,128)S(1)}, f32[2,8,256]{2,1,0:T(8,128)S(1)}) custom-call(s32[1]{0:T(128)} %bitcast.core_ref, f32[512,256]{1,0:T(8,128)S(1)} %bitcast.10, f32[512,256]{1,0:T(8,128)S(1)} %collective-permute-done.1.other_ref, bf16[16,64,512]{2,1,0:T(8,128)(2,1)S(1)} %all-to-all-done.clips_ref), custom_call_target="tpu_custom_call" | custom-call | tf_op jit(solution)/shard_map/pallas_call | solution.py:112
  121.2 5.3 %all-to-all-start.4 = ((bf16[16,32,512]{2,1,0:T(8,128)(2,1)}), bf16[16,32,512]{2,1,0:T(8,128)(2,1)S(1)}, u32[]{:S(2)}, u32[]{:S(2)}) async-start(bf16[16,32,512]{2,1,0:T(8,128)(2,1)} %bitcast.4), calls=%async_computation.4 | async-start | bytes 1048576 | tf_op jit(solution)/shard_map/all_to_all | solution.py:124
  126.5 0.6 slice.6
  127.0 0.6 dynamic_slice.3
  127.6 14.5 %all-to-all-done.4 = bf16[16,32,512]{2,1,0:T(8,128)(2,1)S(1)} async-done(((bf16[16,32,512]{2,1,0:T(8,128)(2,1)}), bf16[16,32,512]{2,1,0:T(8,128)(2,1)S(1)}, u32[]{:S(2)}, u32[]{:S(2)}) %all-to-all-start.4) | async-done | bytes 524320 | tf_op jit(solution)/shard_map/all_to_all | solution.py:124
  142.1 1.1 copy.10
  (1 shorter events, 0.0 us)
Async XLA Ops:
  0.6 1.4 copy-start
  3.4 35.6 %all-to-all-start = ((bf16[16,64,512]{2,1,0:T(8,128)(2,1)}), bf16[16,64,512]{2,1,0:T(8,128)(2,1)S(1)}, u32[]{:S(2)}, u32[]{:S(2)}) async-start(bf16[16,64,512]{2,1,0:T(8,128)(2,1)} %maximum_bitcast_fusion), calls=%async_computation | async-start | bytes 2097152 | tf_op jit(solution)/shard_map/all_to_all | solution.py:88
  39.6 3.8 %collective-permute-start = (f32[512,256]{1,0:T(8,128)S(1)}, f32[512,256]{1,0:T(8,128)S(1)}, u32[]{:S(2)}, u32[]{:S(2)}) collective-permute-start(f32[512,256]{1,0:T(8,128)S(1)} %get-tuple-element.9), channel_id=1, source_target_pairs={{0,1},{1,0},{2,3},{3,2},{4,5},{5,4},{6,7},{7,6},{8,9},{9,8},{10,11... | collective-permute-start | bytes 1572872 | tf_op jit(solution)/shard_map/ppermute | solution.py:98
  113.8 3.8 %collective-permute-start.1 = (f32[512,256]{1,0:T(8,128)S(1)}, f32[512,256]{1,0:T(8,128)S(1)}, u32[]{:S(2)}, u32[]{:S(2)}) collective-permute-start(f32[512,256]{1,0:T(8,128)S(1)} %bitcast.9), channel_id=1, source_target_pairs={{0,1},{1,0},{2,3},{3,2},{4,5},{5,4},{6,7},{7,6},{8,9},{9,8},{10,11... | collective-permute-start | bytes 1572872 | tf_op jit(solution)/shard_map/ppermute | solution.py:110
  121.2 20.9 %all-to-all-start.4 = ((bf16[16,32,512]{2,1,0:T(8,128)(2,1)}), bf16[16,32,512]{2,1,0:T(8,128)(2,1)S(1)}, u32[]{:S(2)}, u32[]{:S(2)}) async-start(bf16[16,32,512]{2,1,0:T(8,128)(2,1)} %bitcast.4), calls=%async_computation.4 | async-start | bytes 1048576 | tf_op jit(solution)/shard_map/all_to_all | solution.py:124

commit v2 on v1

--- a/solution.py
+++ b/solution.py
@@ -6,14 +6,24 @@
 from jax import lax
 from jax.experimental import pallas as pl
 from jax.experimental.pallas import tpu as pltpu
-from jax.sharding import PartitionSpec as P
+from jax.sharding import Mesh, PartitionSpec as P
 
 ITERS = 4
 BLUR = 0.5
 CORES = 2
+FINE = {"z": 2, "q": 4, "p": 2, "h": 4, "x": 4, "c": 2}
+DP = ("z", "q", "p")
+SEQ = ("h", "x", "c")
+NEAR = ("x", "z", "p")
 VMEM = pl.BlockSpec(memory_space=pltpu.VMEM)
 SMEM = pl.BlockSpec(memory_space=pltpu.SMEM)
 LIMIT = pltpu.CompilerParams(vmem_limit_bytes=32 * 1024 * 1024)
+
+
+def pack_kernel(noise_ref, latents_ref, out_ref):
+    local = noise_ref.shape[0]
+    out_ref[:, :local, :] = jnp.swapaxes(noise_ref[...], 0, 1)
+    out_ref[:, local:, :] = jnp.swapaxes(latents_ref[...], 0, 1)
 
 
 def pair_kernel(core_ref, clips_ref, send_ref, keep_ref):
@@ -37,6 +47,20 @@
 
 def spread_kernel(parts_ref, out_ref):
     out_ref[...] = jnp.broadcast_to(jnp.sum(parts_ref[...], axis=0)[None], out_ref.shape)
+
+
+def spread(parts, copies):
+    return pl.pallas_call(
+        spread_kernel,
+        out_shape=jax.ShapeDtypeStruct((copies, *parts.shape[1:]), parts.dtype),
+        in_specs=[VMEM],
+        out_specs=VMEM,
+        compiler_params=LIMIT,
+    )(parts)
+
+
+def exchange(blocks, axes):
+    return lax.all_to_all(blocks, axes, 0, 0, tiled=True)
 
 
 def coupling_kernel(factor, core_ref, own_ref, other_ref, clips_ref, moved_ref, row_ref, column_ref, *scores):
@@ -75,17 +99,21 @@
 
 def per_device(latents, noise):
     local, channels, width = latents.shape
-    dp, seq = lax.axis_size("dp"), lax.axis_size("seq")
+    dp, seq, near = lax.axis_size(DP), lax.axis_size(SEQ), lax.axis_size(NEAR)
     total = local * dp
     half = total // CORES
     factor = math.log2(math.e) / (BLUR * math.sqrt(channels * width * seq))
-    core = lax.rem(lax.axis_index("seq"), CORES)
-    core_scalar = core.reshape(1).astype(jnp.int32)
-    swap = [(i, i ^ 1) for i in range(seq)]
-    chips = [list(range(c, seq, CORES)) for c in range(CORES)]
+    core = lax.axis_index("c").reshape(1).astype(jnp.int32)
+    swap = [(0, 1), (1, 0)]
 
-    packed = jnp.concatenate([noise, latents], axis=0).swapaxes(0, 1)
-    clips = lax.all_to_all(packed, "dp", 0, 0, tiled=True)
+    packed = pl.pallas_call(
+        pack_kernel,
+        out_shape=jax.ShapeDtypeStruct((channels, 2 * local, width), noise.dtype),
+        in_specs=[VMEM, VMEM],
+        out_specs=VMEM,
+        compiler_params=LIMIT,
+    )(noise, latents)
+    clips = exchange(packed, DP)
 
     block = jax.ShapeDtypeStruct((total, half), jnp.float32)
     send, keep = pl.pallas_call(
@@ -94,20 +122,14 @@
         in_specs=[SMEM, VMEM],
         out_specs=(VMEM, VMEM),
         compiler_params=LIMIT,
-    )(core_scalar, clips)
-    summed = keep + lax.ppermute(send, "seq", swap)
+    )(core, clips)
+    summed = keep + lax.ppermute(send, "c", swap)
 
-    spread = pl.pallas_call(
-        spread_kernel,
-        out_shape=jax.ShapeDtypeStruct((dp, local, half), jnp.float32),
-        in_specs=[VMEM],
-        out_specs=VMEM,
-        compiler_params=LIMIT,
-    )
-    parts = lax.all_to_all(summed.reshape(dp, local, half), "dp", 0, 0, tiled=True)
-    parts = lax.all_to_all(spread(parts), "seq", 0, 0, tiled=True, axis_index_groups=chips)
-    own = lax.all_to_all(spread(parts), "dp", 0, 0, tiled=True).reshape(total, half)
-    other = lax.ppermute(own, "seq", swap)
+    parts = exchange(summed.reshape(near, total // near, half), NEAR)
+    parts = exchange(spread(parts, lax.axis_size("h")), "h")
+    parts = exchange(spread(parts, lax.axis_size("q")), "q")
+    own = exchange(spread(parts, near), NEAR).reshape(total, half)
+    other = lax.ppermute(own, "c", swap)
 
     moved, row, column = pl.pallas_call(
         functools.partial(coupling_kernel, factor),
@@ -120,18 +142,18 @@
         out_specs=(VMEM, VMEM, VMEM),
         scratch_shapes=[pltpu.VMEM((total, half), jnp.float32)] * CORES,
         compiler_params=LIMIT,
-    )(core_scalar, own, other, clips)
-    back = lax.all_to_all(moved.reshape(dp, local, width), "dp", 0, 0, tiled=True)
-    targets = back.swapaxes(0, 1)
+    )(core, own, other, clips)
+    targets = exchange(moved.reshape(dp, local, width), DP).swapaxes(0, 1)
     column = lax.dynamic_slice(
-        column[:, 0, :].reshape(total), (lax.axis_index("dp") * local,), (local,)
+        column[:, 0, :].reshape(total), (lax.axis_index(DP) * local,), (local,)
     )
     return (targets, row[0], column)
 
 
 def solution(mesh):
-    in_specs = (P("dp", None, "seq"), P("dp", None, "seq"))
-    out_specs = (P("dp", None, "seq"), P(), P("dp"))
+    fine = Mesh(mesh.devices.reshape(tuple(FINE.values())), tuple(FINE))
+    in_specs = (P(DP, None, SEQ), P(DP, None, SEQ))
+    out_specs = (P(DP, None, SEQ), P(), P(DP))
     return jax.shard_map(
-        per_device, mesh=mesh, in_specs=in_specs, out_specs=out_specs, check_vma=False
+        per_device, mesh=fine, in_specs=in_specs, out_specs=out_specs, check_vma=False
     )

time: 144 us -> 131 us (0.910)
  blocking collectives: 70.3 us -> 58.3 us
    all_to_all x3 -> x4, blocking collectives: 70.3 us -> 58.3 us  [exchange(): return lax.all_to_all(blocks, axes, 0, 0, tiled=True)]
where the time goes in v2:
time: 131 us
  blocking collectives  58.3 us (45%)
  waiting for transfers between devices  44.8 us (34%)
  starting transfers between devices  17.2 us (13%)
  Pallas kernels  5.4 us (4%)
  local copies, waits for them, and re-layouts  4.33 us (3%)
    all_to_all x4, blocking collectives, exchange(): return lax.all_to_all(blocks, axes, 0, 0, tiled=True)  58.3 us
    all_to_all x2, waiting for transfers between devices, exchange(): return lax.all_to_all(blocks, axes, 0, 0, tiled=True)  41 us
    all_to_all x2, starting transfers between devices, exchange(): return lax.all_to_all(blocks, axes, 0, 0, tiled=True)  13.4 us
    pallas_call x1, Pallas kernels, per_device(): pl.pallas_call(functools.partial(coupling_kernel, factor), out_shape=(jax...  3.55 us
    unnamed x5, local copies, waits for them, and re-layouts  3.16 us
  transfers between devices with their start and end apart: 4, of which 4 were waited for; matrix products, arithmetic and copies ran while one was open for 1% of the time, Pallas kernels for 0%

profile of v2, /device:TPU:8, one launch (start us, length us, event | category | flops | bytes accessed | tf_op | source)
XLA Modules:
  0.0 130.8 jit_solution(12924288572453048455)
XLA Ops:
  0.6 0.0 copy-start
  0.6 1.0 copy-done
  1.7 0.0 copy-start.1
  1.7 1.0 copy-done.1
  2.7 1.2 shard_map.49
  3.9 9.4 %all-to-all-start = ((bf16[16,64,512]{2,1,0:T(8,128)(2,1)}), bf16[16,64,512]{2,1,0:T(8,128)(2,1)S(1)}, u32[]{:S(2)}, u32[]{:S(2)}) async-start(bf16[16,64,512]{2,1,0:T(8,128)(2,1)} %shard_map.49), calls=%async_computation | async-start | bytes 2097152 | tf_op jit(solution)/shard_map/all_to_all | solution.py:63
  13.3 26.3 %all-to-all-done.clips_ref = bf16[16,64,512]{2,1,0:T(8,128)(2,1)S(1)} async-done(((bf16[16,64,512]{2,1,0:T(8,128)(2,1)}), bf16[16,64,512]{2,1,0:T(8,128)(2,1)S(1)}, u32[]{:S(2)}, u32[]{:S(2)}) %all-to-all-start) | async-done | bytes 1048608 | tf_op jit(solution)/shard_map/all_to_all | solution.py:63
  39.6 0.5 shard_map.50
  40.1 1.9 %collective-permute-start = (f32[512,256]{1,0:T(8,128)S(1)}, f32[512,256]{1,0:T(8,128)S(1)}, u32[]{:S(2)}, u32[]{:S(2)}) collective-permute-start(f32[512,256]{1,0:T(8,128)S(1)} %get-tuple-element.9), channel_id=1, source_target_pairs={{0,1},{1,0},{2,3},{3,2},{4,5},{5,4},{6,7},{7,6},{8,9},{9,8},{10,11... | collective-permute-start | bytes 1572872 | tf_op jit(solution)/shard_map/ppermute | solution.py:126
  42.0 1.9 %collective-permute-done = f32[512,256]{1,0:T(8,128)S(1)} collective-permute-done((f32[512,256]{1,0:T(8,128)S(1)}, f32[512,256]{1,0:T(8,128)S(1)}, u32[]{:S(2)}, u32[]{:S(2)}) %collective-permute-start) | collective-permute-done | bytes 524320 | tf_op jit(solution)/shard_map/ppermute | solution.py:126
  43.9 0.1 add.12
  44.0 15.9 %all_to_all.30.parts_ref = f32[16,32,256]{2,1,0:T(8,128)S(1)} all-to-all(f32[16,32,256]{2,1,0:T(8,128)S(1)} %bitcast.9), channel_id=1, replica_groups=mesh['z'=2,'q'=4,'p'=2,'h'=4,'x'=4,'c'=2] {'x','z','p'}, dimensions={0} | all-to-all | bytes 1048576 | tf_op jit(solution)/shard_map/all_to_all | solution.py:63
  59.9 18.1 %all_to_all.31.parts_ref = f32[4,32,256]{2,1,0:T(8,128)S(1)} all-to-all(f32[4,32,256]{2,1,0:T(8,128)S(1)} %shard_map.51), channel_id=1, replica_groups=mesh['z'=2,'q'=4,'p'=2,'h'=4,'x'=4,'c'=2] {'h'}, dimensions={0} | all-to-all | bytes 262144 | tf_op jit(solution)/shard_map/all_to_all | solution.py:63
  78.0 12.4 %all_to_all.32.parts_ref = f32[4,32,256]{2,1,0:T(8,128)S(1)} all-to-all(f32[4,32,256]{2,1,0:T(8,128)S(1)} %shard_map.52), channel_id=1, replica_groups=mesh['z'=2,'q'=4,'p'=2,'h'=4,'x'=4,'c'=2] {'q'}, dimensions={0} | all-to-all | bytes 262144 | tf_op jit(solution)/shard_map/all_to_all | solution.py:63
  90.4 11.9 %all_to_all.33 = f32[16,32,256]{2,1,0:T(8,128)S(1)} all-to-all(f32[16,32,256]{2,1,0:T(8,128)S(1)} %shard_map.53), channel_id=1, replica_groups=mesh['z'=2,'q'=4,'p'=2,'h'=4,'x'=4,'c'=2] {'x','z','p'}, dimensions={0} | all-to-all | bytes 1048576 | tf_op jit(solution)/shard_map/all_to_all | solution.py:63
  102.4 1.9 %collective-permute-start.1 = (f32[512,256]{1,0:T(8,128)S(1)}, f32[512,256]{1,0:T(8,128)S(1)}, u32[]{:S(2)}, u32[]{:S(2)}) collective-permute-start(f32[512,256]{1,0:T(8,128)S(1)} %bitcast.7), channel_id=1, source_target_pairs={{0,1},{1,0},{2,3},{3,2},{4,5},{5,4},{6,7},{7,6},{8,9},{9,8},{10,11... | collective-permute-start | bytes 1572872 | tf_op jit(solution)/shard_map/ppermute | solution.py:132
  104.3 1.9 %collective-permute-done.1.other_ref = f32[512,256]{1,0:T(8,128)S(1)} collective-permute-done((f32[512,256]{1,0:T(8,128)S(1)}, f32[512,256]{1,0:T(8,128)S(1)}, u32[]{:S(2)}, u32[]{:S(2)}) %collective-permute-start.1) | collective-permute-done | bytes 524320 | tf_op jit(solution)/shard_map/ppermute | solution.py:132
  106.2 3.6 %shard_map.54 = (bf16[2,256,512]{2,1,0:T(8,128)(2,1)}, f32[8,512]{1,0:T(8,128)S(1)}, f32[2,8,256]{2,1,0:T(8,128)S(1)}) custom-call(s32[1]{0:T(128)} %bitcast.core_ref, f32[512,256]{1,0:T(8,128)S(1)} %bitcast.8, f32[512,256]{1,0:T(8,128)S(1)} %collective-permute-done.1.other_ref, bf16[16,64,512]{2,1,0:T(8,128)(2,1)S(1)} %all-to-all-done.clips_ref), custom_call_target="tpu_custom_call" | custom-call | tf_op jit(solution)/shard_map/pallas_call | solution.py:134
  109.7 4.0 %all-to-all-start.5 = ((bf16[16,32,512]{2,1,0:T(8,128)(2,1)}), bf16[16,32,512]{2,1,0:T(8,128)(2,1)S(1)}, u32[]{:S(2)}, u32[]{:S(2)}) async-start(bf16[16,32,512]{2,1,0:T(8,128)(2,1)} %bitcast.3), calls=%async_computation.5 | async-start | bytes 1048576 | tf_op jit(solution)/shard_map/all_to_all | solution.py:63
  113.7 0.6 slice.6
  114.3 0.6 dynamic_slice.3
  114.9 14.8 %all-to-all-done.5 = bf16[16,32,512]{2,1,0:T(8,128)(2,1)S(1)} async-done(((bf16[16,32,512]{2,1,0:T(8,128)(2,1)}), bf16[16,32,512]{2,1,0:T(8,128)(2,1)S(1)}, u32[]{:S(2)}, u32[]{:S(2)}) %all-to-all-start.5) | async-done | bytes 524320 | tf_op jit(solution)/shard_map/all_to_all | solution.py:63
  129.7 1.1 copy.6
  (4 shorter events, 0.1 us)
Async XLA Ops:
  0.6 1.0 copy-start
  1.7 1.0 copy-start.1
  3.9 35.6 %all-to-all-start = ((bf16[16,64,512]{2,1,0:T(8,128)(2,1)}), bf16[16,64,512]{2,1,0:T(8,128)(2,1)S(1)}, u32[]{:S(2)}, u32[]{:S(2)}) async-start(bf16[16,64,512]{2,1,0:T(8,128)(2,1)} %shard_map.49), calls=%async_computation | async-start | bytes 2097152 | tf_op jit(solution)/shard_map/all_to_all | solution.py:63
  40.1 3.8 %collective-permute-start = (f32[512,256]{1,0:T(8,128)S(1)}, f32[512,256]{1,0:T(8,128)S(1)}, u32[]{:S(2)}, u32[]{:S(2)}) collective-permute-start(f32[512,256]{1,0:T(8,128)S(1)} %get-tuple-element.9), channel_id=1, source_target_pairs={{0,1},{1,0},{2,3},{3,2},{4,5},{5,4},{6,7},{7,6},{8,9},{9,8},{10,11... | collective-permute-start | bytes 1572872 | tf_op jit(solution)/shard_map/ppermute | solution.py:126
  102.4 3.8 %collective-permute-start.1 = (f32[512,256]{1,0:T(8,128)S(1)}, f32[512,256]{1,0:T(8,128)S(1)}, u32[]{:S(2)}, u32[]{:S(2)}) collective-permute-start(f32[512,256]{1,0:T(8,128)S(1)} %bitcast.7), channel_id=1, source_target_pairs={{0,1},{1,0},{2,3},{3,2},{4,5},{5,4},{6,7},{7,6},{8,9},{9,8},{10,11... | collective-permute-start | bytes 1572872 | tf_op jit(solution)/shard_map/ppermute | solution.py:132
  109.7 20.0 %all-to-all-start.5 = ((bf16[16,32,512]{2,1,0:T(8,128)(2,1)}), bf16[16,32,512]{2,1,0:T(8,128)(2,1)S(1)}, u32[]{:S(2)}, u32[]{:S(2)}) async-start(bf16[16,32,512]{2,1,0:T(8,128)(2,1)} %bitcast.3), calls=%async_computation.5 | async-start | bytes 1048576 | tf_op jit(solution)/shard_map/all_to_all | solution.py:63

commit v3 on v2

--- a/solution.py
+++ b/solution.py
@@ -15,15 +15,24 @@
 DP = ("z", "q", "p")
 SEQ = ("h", "x", "c")
 NEAR = ("x", "z", "p")
+ANY = pl.BlockSpec(memory_space=pl.ANY)
 VMEM = pl.BlockSpec(memory_space=pltpu.VMEM)
 SMEM = pl.BlockSpec(memory_space=pltpu.SMEM)
+WHOLE = pltpu.CompilerParams(vmem_limit_bytes=60 * 1024 * 1024)
 LIMIT = pltpu.CompilerParams(vmem_limit_bytes=32 * 1024 * 1024)
 
 
-def pack_kernel(noise_ref, latents_ref, out_ref):
+def pack_kernel(noise_ref, latents_ref, out_ref, held, arrived):
     local = noise_ref.shape[0]
-    out_ref[:, :local, :] = jnp.swapaxes(noise_ref[...], 0, 1)
-    out_ref[:, local:, :] = jnp.swapaxes(latents_ref[...], 0, 1)
+    copies = [
+        pltpu.make_async_copy(given, held.at[k], arrived.at[k])
+        for k, given in enumerate((noise_ref, latents_ref))
+    ]
+    for copy in copies:
+        copy.start()
+    for k, copy in enumerate(copies):
+        copy.wait()
+        out_ref[:, k * local : (k + 1) * local, :] = jnp.swapaxes(held[k], 0, 1)
 
 
 def pair_kernel(core_ref, clips_ref, send_ref, keep_ref):
@@ -63,7 +72,7 @@
     return lax.all_to_all(blocks, axes, 0, 0, tiled=True)
 
 
-def coupling_kernel(factor, core_ref, own_ref, other_ref, clips_ref, moved_ref, row_ref, column_ref, *scores):
+def coupling_kernel(factor, core_ref, group_ref, own_ref, other_ref, clips_ref, moved_ref, row_ref, column_ref, *scores):
     sources, both, width = clips_ref.shape
     local = both // 2
     core = core_ref[0]
@@ -85,7 +94,12 @@
         row = log_mass - (top + jnp.log2(mass))
     noise = clips_ref[:, :local, :].reshape(total, width)
     back = BLUR * math.log(2.0)
-    row_ref[...] = jnp.transpose(jnp.broadcast_to(row * back, (total, 128)))[:8, :]
+    row_ref[...] = jnp.transpose(jnp.broadcast_to(row * back, (total, 128)))[:1, :]
+    group = group_ref[0]
+    half = total // CORES
+    column = jnp.where(group * local // half == core, *columns) * back
+    column = pltpu.roll(column, lax.rem(half - lax.rem(group * local, half), half), 1)
+    column_ref[...] = column[:, :local]
     for k, (column, score) in enumerate(zip(columns, scores, strict=True)):
         place = core if k == 0 else 1 - core
         plan = jnp.exp2((row + column) - score[...])
@@ -94,7 +108,6 @@
             weights, noise, (((0,), (0,)), ((), ())), preferred_element_type=jnp.float32
         )
         moved_ref[place] = moved.astype(jnp.bfloat16)
-        column_ref[place] = jnp.broadcast_to(column * back, column_ref.shape[1:])
 
 
 def per_device(latents, noise):
@@ -104,15 +117,21 @@
     half = total // CORES
     factor = math.log2(math.e) / (BLUR * math.sqrt(channels * width * seq))
     core = lax.axis_index("c").reshape(1).astype(jnp.int32)
+    group = lax.axis_index(DP).reshape(1).astype(jnp.int32)
     swap = [(0, 1), (1, 0)]
 
     packed = pl.pallas_call(
         pack_kernel,
         out_shape=jax.ShapeDtypeStruct((channels, 2 * local, width), noise.dtype),
-        in_specs=[VMEM, VMEM],
+        in_specs=[ANY, ANY],
         out_specs=VMEM,
-        compiler_params=LIMIT,
+        scratch_shapes=[
+            pltpu.VMEM((2, *noise.shape), noise.dtype),
+            pltpu.SemaphoreType.DMA((2,)),
+        ],
+        compiler_params=WHOLE,
     )(noise, latents)
+    packed, core, group = lax.optimization_barrier((packed, core, group))
     clips = exchange(packed, DP)
 
     block = jax.ShapeDtypeStruct((total, half), jnp.float32)
@@ -135,19 +154,16 @@
         functools.partial(coupling_kernel, factor),
         out_shape=(
             jax.ShapeDtypeStruct((CORES, half, width), jnp.bfloat16),
-            jax.ShapeDtypeStruct((8, total), jnp.float32),
-            jax.ShapeDtypeStruct((CORES, 8, half), jnp.float32),
+            jax.ShapeDtypeStruct((1, total), jnp.float32),
+            jax.ShapeDtypeStruct((1, local), jnp.float32),
         ),
-        in_specs=[SMEM, VMEM, VMEM, VMEM],
+        in_specs=[SMEM, SMEM, VMEM, VMEM, VMEM],
         out_specs=(VMEM, VMEM, VMEM),
         scratch_shapes=[pltpu.VMEM((total, half), jnp.float32)] * CORES,
         compiler_params=LIMIT,
-    )(core, own, other, clips)
+    )(core, group, own, other, clips)
     targets = exchange(moved.reshape(dp, local, width), DP).swapaxes(0, 1)
-    column = lax.dynamic_slice(
-        column[:, 0, :].reshape(total), (lax.axis_index(DP) * local,), (local,)
-    )
-    return (targets, row[0], column)
+    return (targets, row.reshape(total), column.reshape(local))
 
 
 def solution(mesh):

time: 131 us -> 129 us (0.985)
  blocking collectives: 58.3 us -> 113 us
  waiting for transfers between devices: 44.8 us -> 3.75 us
  starting transfers between devices: 17.2 us -> 3.83 us
  local copies, waits for them, and re-layouts: 4.33 us -> 1.09 us
    all_to_all x4 -> x6, blocking collectives: 58.3 us -> 113 us  [exchange(): return lax.all_to_all(blocks, axes, 0, 0, tiled=True)]
    all_to_all x2 -> x0, waiting for transfers between devices: 41 us -> none  [exchange(): return lax.all_to_all(blocks, axes, 0, 0, tiled=True)]
    all_to_all x2 -> x0, starting transfers between devices: 13.4 us -> none  [exchange(): return lax.all_to_all(blocks, axes, 0, 0, tiled=True)]
    unnamed x5 -> x1, local copies, waits for them, and re-layouts: 3.16 us -> 1.09 us
  transfers between devices with their start and end apart: 4 -> 2, of which waited for: 4 -> 2; matrix products, arithmetic and copies ran while one was open for 1% -> 0% of each run, Pallas kernels for 0% -> 0%
where the time goes in v3:
time: 129 us
  blocking collectives  113 us (88%)
  Pallas kernels  6.17 us (5%)
  starting transfers between devices  3.83 us (3%)
  waiting for transfers between devices  3.75 us (3%)
    all_to_all x6, blocking collectives, exchange(): return lax.all_to_all(blocks, axes, 0, 0, tiled=True)  113 us
    pallas_call x1, Pallas kernels, per_device(): pl.pallas_call(functools.partial(coupling_kernel, factor), out_shape=(jax...  3.23 us
  transfers between devices with their start and end apart: 2, of which 2 were waited for; matrix products, arithmetic and copies ran while one was open for 0% of the time, Pallas kernels for 0%

profile of v3, /device:TPU:8, one launch (start us, length us, event | category | flops | bytes accessed | tf_op | source)
XLA Modules:
  0.0 128.6 jit_solution(945522107078180868)
XLA Ops:
  0.6 2.3 %shard_map.49 = bf16[16,64,512]{2,1,0:T(8,128)(2,1)} custom-call(bf16[32,16,512]{2,1,0:T(8,128)(2,1)} %noise_ref.1, bf16[32,16,512]{2,1,0:T(8,128)(2,1)} %latents_ref.1), custom_call_target="tpu_custom_call" | custom-call | tf_op jit(solution)/shard_map/pallas_call | solution.py:123
  3.0 35.6 %all_to_all.30.clips_ref = bf16[16,64,512]{2,1,0:T(8,128)(2,1)S(1)} all-to-all(bf16[16,64,512]{2,1,0:T(8,128)(2,1)} %shard_map.49), channel_id=1, replica_groups=mesh['z'=2,'q'=4,'p'=2,'h'=4,'x'=4,'c'=2] {'z','q','p'}, dimensions={0} | all-to-all | bytes 2097152 | tf_op jit(solution)/shard_map/all_to_all | solution.py:72
  38.5 0.5 shard_map.50
  39.1 1.9 %collective-permute-start = (f32[512,256]{1,0:T(8,128)S(1)}, f32[512,256]{1,0:T(8,128)S(1)}, u32[]{:S(2)}, u32[]{:S(2)}) collective-permute-start(f32[512,256]{1,0:T(8,128)S(1)} %get-tuple-element.15), channel_id=1, source_target_pairs={{0,1},{1,0},{2,3},{3,2},{4,5},{5,4},{6,7},{7,6},{8,9},{9,8},{10,11... | collective-permute-start | bytes 1572872 | tf_op jit(solution)/shard_map/ppermute | solution.py:145
  41.0 1.9 %collective-permute-done = f32[512,256]{1,0:T(8,128)S(1)} collective-permute-done((f32[512,256]{1,0:T(8,128)S(1)}, f32[512,256]{1,0:T(8,128)S(1)}, u32[]{:S(2)}, u32[]{:S(2)}) %collective-permute-start) | collective-permute-done | bytes 524320 | tf_op jit(solution)/shard_map/ppermute | solution.py:145
  42.9 0.1 add.11
  43.0 16.1 %all_to_all.31.parts_ref = f32[16,32,256]{2,1,0:T(8,128)S(1)} all-to-all(f32[16,32,256]{2,1,0:T(8,128)S(1)} %bitcast.11), channel_id=1, replica_groups=mesh['z'=2,'q'=4,'p'=2,'h'=4,'x'=4,'c'=2] {'x','z','p'}, dimensions={0} | all-to-all | bytes 1048576 | tf_op jit(solution)/shard_map/all_to_all | solution.py:72
  59.1 18.1 %all_to_all.32.parts_ref = f32[4,32,256]{2,1,0:T(8,128)S(1)} all-to-all(f32[4,32,256]{2,1,0:T(8,128)S(1)} %shard_map.51), channel_id=1, replica_groups=mesh['z'=2,'q'=4,'p'=2,'h'=4,'x'=4,'c'=2] {'h'}, dimensions={0} | all-to-all | bytes 262144 | tf_op jit(solution)/shard_map/all_to_all | solution.py:72
  77.3 11.8 %all_to_all.33.parts_ref = f32[4,32,256]{2,1,0:T(8,128)S(1)} all-to-all(f32[4,32,256]{2,1,0:T(8,128)S(1)} %shard_map.52), channel_id=1, replica_groups=mesh['z'=2,'q'=4,'p'=2,'h'=4,'x'=4,'c'=2] {'q'}, dimensions={0} | all-to-all | bytes 262144 | tf_op jit(solution)/shard_map/all_to_all | solution.py:72
  89.1 11.9 %all_to_all.34 = f32[16,32,256]{2,1,0:T(8,128)S(1)} all-to-all(f32[16,32,256]{2,1,0:T(8,128)S(1)} %shard_map.53), channel_id=1, replica_groups=mesh['z'=2,'q'=4,'p'=2,'h'=4,'x'=4,'c'=2] {'x','z','p'}, dimensions={0} | all-to-all | bytes 1048576 | tf_op jit(solution)/shard_map/all_to_all | solution.py:72
  101.1 1.9 %collective-permute-start.1 = (f32[512,256]{1,0:T(8,128)S(1)}, f32[512,256]{1,0:T(8,128)S(1)}, u32[]{:S(2)}, u32[]{:S(2)}) collective-permute-start(f32[512,256]{1,0:T(8,128)S(1)} %bitcast.8), channel_id=1, source_target_pairs={{0,1},{1,0},{2,3},{3,2},{4,5},{5,4},{6,7},{7,6},{8,9},{9,8},{10,11... | collective-permute-start | bytes 1572872 | tf_op jit(solution)/shard_map/ppermute | solution.py:151
  103.0 1.9 %collective-permute-done.1.other_ref = f32[512,256]{1,0:T(8,128)S(1)} collective-permute-done((f32[512,256]{1,0:T(8,128)S(1)}, f32[512,256]{1,0:T(8,128)S(1)}, u32[]{:S(2)}, u32[]{:S(2)}) %collective-permute-start.1) | collective-permute-done | bytes 524320 | tf_op jit(solution)/shard_map/ppermute | solution.py:151
  104.8 3.2 %shard_map.54 = (bf16[2,256,512]{2,1,0:T(8,128)(2,1)S(1)}, f32[1,512]{1,0:T(1,128)}, f32[1,32]{1,0:T(1,128)}) custom-call(s32[1]{0:T(128)} %bitcast.core_ref, s32[1]{0:T(128)} %bitcast.1.group_ref, f32[512,256]{1,0:T(8,128)S(1)} %bitcast.9, f32[512,256]{1,0:T(8,128)S(1)} %collective-permute-done.1.other_ref, bf16[16,64,512]{2,1,0:T(8,128)(2,1)S(1)} %all_to_all.30.clips_ref), custom_call_target="tpu_custom_call" | custom-call | tf_op jit(solution)/shard_map/pallas_call | solution.py:153
  108.1 19.4 %all_to_all.35 = bf16[16,32,512]{2,1,0:T(8,128)(2,1)S(1)} all-to-all(bf16[16,32,512]{2,1,0:T(8,128)(2,1)S(1)} %bitcast.10), channel_id=1, replica_groups=mesh['z'=2,'q'=4,'p'=2,'h'=4,'x'=4,'c'=2] {'z','q','p'}, dimensions={0} | all-to-all | bytes 1048576 | tf_op jit(solution)/shard_map/all_to_all | solution.py:72
  127.5 1.1 copy.6
  (3 shorter events, 0.1 us)
Async XLA Ops:
  39.1 3.8 %collective-permute-start = (f32[512,256]{1,0:T(8,128)S(1)}, f32[512,256]{1,0:T(8,128)S(1)}, u32[]{:S(2)}, u32[]{:S(2)}) collective-permute-start(f32[512,256]{1,0:T(8,128)S(1)} %get-tuple-element.15), channel_id=1, source_target_pairs={{0,1},{1,0},{2,3},{3,2},{4,5},{5,4},{6,7},{7,6},{8,9},{9,8},{10,11... | collective-permute-start | bytes 1572872 | tf_op jit(solution)/shard_map/ppermute | solution.py:145
  101.1 3.8 %collective-permute-start.1 = (f32[512,256]{1,0:T(8,128)S(1)}, f32[512,256]{1,0:T(8,128)S(1)}, u32[]{:S(2)}, u32[]{:S(2)}) collective-permute-start(f32[512,256]{1,0:T(8,128)S(1)} %bitcast.8), channel_id=1, source_target_pairs={{0,1},{1,0},{2,3},{3,2},{4,5},{5,4},{6,7},{7,6},{8,9},{9,8},{10,11... | collective-permute-start | bytes 1572872 | tf_op jit(solution)/shard_map/ppermute | solution.py:151

commit v4 on v3

--- a/solution.py
+++ b/solution.py
@@ -15,10 +15,9 @@
 DP = ("z", "q", "p")
 SEQ = ("h", "x", "c")
 NEAR = ("x", "z", "p")
-ANY = pl.BlockSpec(memory_space=pl.ANY)
+HBM = pl.BlockSpec(memory_space=pltpu.HBM)
 VMEM = pl.BlockSpec(memory_space=pltpu.VMEM)
 SMEM = pl.BlockSpec(memory_space=pltpu.SMEM)
-WHOLE = pltpu.CompilerParams(vmem_limit_bytes=60 * 1024 * 1024)
 LIMIT = pltpu.CompilerParams(vmem_limit_bytes=32 * 1024 * 1024)
 
 
@@ -123,13 +122,13 @@
     packed = pl.pallas_call(
         pack_kernel,
         out_shape=jax.ShapeDtypeStruct((channels, 2 * local, width), noise.dtype),
-        in_specs=[ANY, ANY],
+        in_specs=[HBM, HBM],
         out_specs=VMEM,
         scratch_shapes=[
             pltpu.VMEM((2, *noise.shape), noise.dtype),
             pltpu.SemaphoreType.DMA((2,)),
         ],
-        compiler_params=WHOLE,
+        compiler_params=LIMIT,
     )(noise, latents)
     packed, core, group = lax.optimization_barrier((packed, core, group))
     clips = exchange(packed, DP)

time: 129 us -> 129 us (level)
  local copies, waits for them, and re-layouts: 1.09 us -> 3.16 us
  Pallas kernels: 6.17 us -> 4.21 us
    unnamed x1 -> x5, local copies, waits for them, and re-layouts: 1.09 us -> 3.16 us
    pallas_call x1, Pallas kernels: 2.31 us -> 0.35 us  [per_device(): pl.pallas_call(pack_kernel, out_shape=jax.ShapeDtypeStruct((channels, 2 *...]
where the time goes in v4:
time: 129 us; the launch traced here: 128 us
  blocking collectives  113 us (88%)
  Pallas kernels  4.21 us (3%)
  starting transfers between devices  3.83 us (3%)
  waiting for transfers between devices  3.75 us (3%)
  local copies, waits for them, and re-layouts  3.16 us (2%)
    all_to_all x6, blocking collectives, exchange(): return lax.all_to_all(blocks, axes, 0, 0, tiled=True)  113 us
    pallas_call x1, Pallas kernels, per_device(): pl.pallas_call(functools.partial(coupling_kernel, factor), out_shape=(jax...  3.23 us
    unnamed x5, local copies, waits for them, and re-layouts  3.16 us
  transfers between devices with their start and end apart: 2, of which 2 were waited for; matrix products, arithmetic and copies ran while one was open for 0% of the time, Pallas kernels for 0%

profile of v4, /device:TPU:8, one launch (start us, length us, event | category | flops | bytes accessed | tf_op | source)
XLA Modules:
  0.0 128.4 jit_solution(13800052941778968000)
XLA Ops:
  0.6 0.0 copy-start
  0.6 1.0 copy-done
  1.7 0.0 copy-start.1
  1.7 1.0 copy-done.1
  2.7 0.3 shard_map.49
  3.1 35.4 %all_to_all.30.clips_ref = bf16[16,64,512]{2,1,0:T(8,128)(2,1)S(1)} all-to-all(bf16[16,64,512]{2,1,0:T(8,128)(2,1)S(1)} %shard_map.49), channel_id=1, replica_groups=mesh['z'=2,'q'=4,'p'=2,'h'=4,'x'=4,'c'=2] {'z','q','p'}, dimensions={0} | all-to-all | bytes 2097152 | tf_op jit(solution)/shard_map/all_to_all | solution.py:71
  38.5 0.5 shard_map.50
  39.0 1.9 %collective-permute-start = (f32[512,256]{1,0:T(8,128)S(1)}, f32[512,256]{1,0:T(8,128)S(1)}, u32[]{:S(2)}, u32[]{:S(2)}) collective-permute-start(f32[512,256]{1,0:T(8,128)S(1)} %get-tuple-element.15), channel_id=1, source_target_pairs={{0,1},{1,0},{2,3},{3,2},{4,5},{5,4},{6,7},{7,6},{8,9},{9,8},{10,11... | collective-permute-start | bytes 1572872 | tf_op jit(solution)/shard_map/ppermute | solution.py:144
  40.9 1.9 %collective-permute-done = f32[512,256]{1,0:T(8,128)S(1)} collective-permute-done((f32[512,256]{1,0:T(8,128)S(1)}, f32[512,256]{1,0:T(8,128)S(1)}, u32[]{:S(2)}, u32[]{:S(2)}) %collective-permute-start) | collective-permute-done | bytes 524320 | tf_op jit(solution)/shard_map/ppermute | solution.py:144
  42.8 0.1 add.11
  42.9 16.1 %all_to_all.31.parts_ref = f32[16,32,256]{2,1,0:T(8,128)S(1)} all-to-all(f32[16,32,256]{2,1,0:T(8,128)S(1)} %bitcast.11), channel_id=1, replica_groups=mesh['z'=2,'q'=4,'p'=2,'h'=4,'x'=4,'c'=2] {'x','z','p'}, dimensions={0} | all-to-all | bytes 1048576 | tf_op jit(solution)/shard_map/all_to_all | solution.py:71
  59.0 18.1 %all_to_all.32.parts_ref = f32[4,32,256]{2,1,0:T(8,128)S(1)} all-to-all(f32[4,32,256]{2,1,0:T(8,128)S(1)} %shard_map.51), channel_id=1, replica_groups=mesh['z'=2,'q'=4,'p'=2,'h'=4,'x'=4,'c'=2] {'h'}, dimensions={0} | all-to-all | bytes 262144 | tf_op jit(solution)/shard_map/all_to_all | solution.py:71
  77.2 11.8 %all_to_all.33.parts_ref = f32[4,32,256]{2,1,0:T(8,128)S(1)} all-to-all(f32[4,32,256]{2,1,0:T(8,128)S(1)} %shard_map.52), channel_id=1, replica_groups=mesh['z'=2,'q'=4,'p'=2,'h'=4,'x'=4,'c'=2] {'q'}, dimensions={0} | all-to-all | bytes 262144 | tf_op jit(solution)/shard_map/all_to_all | solution.py:71
  89.0 11.9 %all_to_all.34 = f32[16,32,256]{2,1,0:T(8,128)S(1)} all-to-all(f32[16,32,256]{2,1,0:T(8,128)S(1)} %shard_map.53), channel_id=1, replica_groups=mesh['z'=2,'q'=4,'p'=2,'h'=4,'x'=4,'c'=2] {'x','z','p'}, dimensions={0} | all-to-all | bytes 1048576 | tf_op jit(solution)/shard_map/all_to_all | solution.py:71
  101.0 1.9 %collective-permute-start.1 = (f32[512,256]{1,0:T(8,128)S(1)}, f32[512,256]{1,0:T(8,128)S(1)}, u32[]{:S(2)}, u32[]{:S(2)}) collective-permute-start(f32[512,256]{1,0:T(8,128)S(1)} %bitcast.8), channel_id=1, source_target_pairs={{0,1},{1,0},{2,3},{3,2},{4,5},{5,4},{6,7},{7,6},{8,9},{9,8},{10,11... | collective-permute-start | bytes 1572872 | tf_op jit(solution)/shard_map/ppermute | solution.py:150
  102.9 1.9 %collective-permute-done.1.other_ref = f32[512,256]{1,0:T(8,128)S(1)} collective-permute-done((f32[512,256]{1,0:T(8,128)S(1)}, f32[512,256]{1,0:T(8,128)S(1)}, u32[]{:S(2)}, u32[]{:S(2)}) %collective-permute-start.1) | collective-permute-done | bytes 524320 | tf_op jit(solution)/shard_map/ppermute | solution.py:150
  104.8 3.2 %shard_map.54 = (bf16[2,256,512]{2,1,0:T(8,128)(2,1)S(1)}, f32[1,512]{1,0:T(1,128)}, f32[1,32]{1,0:T(1,128)}) custom-call(s32[1]{0:T(128)} %bitcast.core_ref, s32[1]{0:T(128)} %bitcast.1.group_ref, f32[512,256]{1,0:T(8,128)S(1)} %bitcast.9, f32[512,256]{1,0:T(8,128)S(1)} %collective-permute-done.1.other_ref, bf16[16,64,512]{2,1,0:T(8,128)(2,1)S(1)} %all_to_all.30.clips_ref), custom_call_target="tpu_custom_call" | custom-call | tf_op jit(solution)/shard_map/pallas_call | solution.py:152
  108.0 19.4 %all_to_all.35 = bf16[16,32,512]{2,1,0:T(8,128)(2,1)S(1)} all-to-all(bf16[16,32,512]{2,1,0:T(8,128)(2,1)S(1)} %bitcast.10), channel_id=1, replica_groups=mesh['z'=2,'q'=4,'p'=2,'h'=4,'x'=4,'c'=2] {'z','q','p'}, dimensions={0} | all-to-all | bytes 1048576 | tf_op jit(solution)/shard_map/all_to_all | solution.py:71
  127.4 1.1 copy.6
  (3 shorter events, 0.1 us)
Async XLA Ops:
  0.6 1.0 copy-start
  1.7 1.0 copy-start.1
  39.0 3.8 %collective-permute-start = (f32[512,256]{1,0:T(8,128)S(1)}, f32[512,256]{1,0:T(8,128)S(1)}, u32[]{:S(2)}, u32[]{:S(2)}) collective-permute-start(f32[512,256]{1,0:T(8,128)S(1)} %get-tuple-element.15), channel_id=1, source_target_pairs={{0,1},{1,0},{2,3},{3,2},{4,5},{5,4},{6,7},{7,6},{8,9},{9,8},{10,11... | collective-permute-start | bytes 1572872 | tf_op jit(solution)/shard_map/ppermute | solution.py:144
  101.0 3.8 %collective-permute-start.1 = (f32[512,256]{1,0:T(8,128)S(1)}, f32[512,256]{1,0:T(8,128)S(1)}, u32[]{:S(2)}, u32[]{:S(2)}) collective-permute-start(f32[512,256]{1,0:T(8,128)S(1)} %bitcast.8), channel_id=1, source_target_pairs={{0,1},{1,0},{2,3},{3,2},{4,5},{5,4},{6,7},{7,6},{8,9},{9,8},{10,11... | collective-permute-start | bytes 1572872 | tf_op jit(solution)/shard_map/ppermute | solution.py:150

commit v5 on v4

--- a/solution.py
+++ b/solution.py
@@ -34,23 +34,23 @@
         out_ref[:, k * local : (k + 1) * local, :] = jnp.swapaxes(held[k], 0, 1)
 
 
-def pair_kernel(core_ref, clips_ref, send_ref, keep_ref):
+def pair_kernel(factor, core_ref, clips_ref, send_ref, keep_ref):
     sources, both, width = clips_ref.shape
     local = both // 2
     half = sources // CORES
     core = core_ref[0]
     noise = clips_ref[:, :local, :].reshape(sources * local, width)
     wide = noise.astype(jnp.float32)
-    noise_norms = jnp.sum(wide * wide, axis=1, keepdims=True)
+    noise_norms = jnp.sum(wide * wide, axis=1, keepdims=True) * factor
     for first, out_ref in ((half * (1 - core), send_ref), (half * core, keep_ref)):
         latents = clips_ref[pl.ds(first, half), local:, :].reshape(half * local, width)
         wide = latents.astype(jnp.float32)
-        latent_norms = jnp.sum(wide * wide, axis=1, keepdims=True)
+        latent_norms = jnp.sum(wide * wide, axis=1, keepdims=True) * factor
         latent_norms = jnp.transpose(jnp.broadcast_to(latent_norms, (half * local, 128)))[:1, :]
         cross = lax.dot_general(
             noise, latents, (((1,), (1,)), ((), ())), preferred_element_type=jnp.float32
         )
-        out_ref[...] = noise_norms + latent_norms - 2.0 * cross
+        out_ref[...] = noise_norms + latent_norms - (2.0 * factor) * cross
 
 
 def spread_kernel(parts_ref, out_ref):
@@ -71,14 +71,13 @@
     return lax.all_to_all(blocks, axes, 0, 0, tiled=True)
 
 
-def coupling_kernel(factor, core_ref, group_ref, own_ref, other_ref, clips_ref, moved_ref, row_ref, column_ref, *scores):
+def coupling_kernel(core_ref, group_ref, own_ref, other_ref, clips_ref, moved_ref, row_ref, column_ref):
+    scores = (own_ref, other_ref)
     sources, both, width = clips_ref.shape
     local = both // 2
     core = core_ref[0]
     total = sources * local
     log_mass = -math.log2(total)
-    for score, given in zip(scores, (own_ref, other_ref), strict=True):
-        score[...] = given[...] * factor
     row = jnp.zeros((total, 1), jnp.float32)
     columns = [None] * CORES
     for step in range(ITERS):
@@ -102,7 +101,7 @@
     for k, (column, score) in enumerate(zip(columns, scores, strict=True)):
         place = core if k == 0 else 1 - core
         plan = jnp.exp2((row + column) - score[...])
-        weights = (plan / jnp.sum(plan, axis=0, keepdims=True)).astype(jnp.bfloat16)
+        weights = (plan * (1.0 / jnp.sum(plan, axis=0, keepdims=True))).astype(jnp.bfloat16)
         moved = lax.dot_general(
             weights, noise, (((0,), (0,)), ((), ())), preferred_element_type=jnp.float32
         )
@@ -129,13 +128,13 @@
             pltpu.SemaphoreType.DMA((2,)),
         ],
         compiler_params=LIMIT,
-    )(noise, latents)
+    )(*(pltpu.with_memory_space_constraint(given, pltpu.HBM) for given in (noise, latents)))
     packed, core, group = lax.optimization_barrier((packed, core, group))
     clips = exchange(packed, DP)
 
     block = jax.ShapeDtypeStruct((total, half), jnp.float32)
     send, keep = pl.pallas_call(
-        pair_kernel,
+        functools.partial(pair_kernel, factor),
         out_shape=(block, block),
         in_specs=[SMEM, VMEM],
         out_specs=(VMEM, VMEM),
@@ -150,7 +149,7 @@
     other = lax.ppermute(own, "c", swap)
 
     moved, row, column = pl.pallas_call(
-        functools.partial(coupling_kernel, factor),
+        coupling_kernel,
         out_shape=(
             jax.ShapeDtypeStruct((CORES, half, width), jnp.bfloat16),
             jax.ShapeDtypeStruct((1, total), jnp.float32),
@@ -158,7 +157,6 @@
         ),
         in_specs=[SMEM, SMEM, VMEM, VMEM, VMEM],
         out_specs=(VMEM, VMEM, VMEM),
-        scratch_shapes=[pltpu.VMEM((total, half), jnp.float32)] * CORES,
         compiler_params=LIMIT,
     )(core, group, own, other, clips)
     targets = exchange(moved.reshape(dp, local, width), DP).swapaxes(0, 1)

time: 129 us -> 128 us (level)
  local copies, waits for them, and re-layouts: 3.16 us -> 1.09 us
    unnamed x5 -> x1, local copies, waits for them, and re-layouts: 3.16 us -> 1.09 us
where the time goes in v5:
time: 128 us; the launch traced here: 127 us
  blocking collectives  113 us (88%)
  Pallas kernels  5.19 us (4%)
  starting transfers between devices  3.83 us (3%)
  waiting for transfers between devices  3.75 us (3%)
    all_to_all x6, blocking collectives, exchange(): return lax.all_to_all(blocks, axes, 0, 0, tiled=True)  113 us
    pallas_call x1, Pallas kernels, per_device(): pl.pallas_call(coupling_kernel, out_shape=(jax.ShapeDtypeStruct((CORES, h...  3.17 us
  transfers between devices with their start and end apart: 2, of which 2 were waited for; matrix products, arithmetic and copies ran while one was open for 0% of the time, Pallas kernels for 0%

profile of v5, /device:TPU:8, one launch (start us, length us, event | category | flops | bytes accessed | tf_op | source)
XLA Modules:
  0.0 127.3 jit_solution(4512222933512425838)
XLA Ops:
  0.6 1.3 %shard_map.49 = bf16[16,64,512]{2,1,0:T(8,128)(2,1)S(1)} custom-call(bf16[32,16,512]{2,1,0:T(8,128)(2,1)} %noise_ref.1, bf16[32,16,512]{2,1,0:T(8,128)(2,1)} %latents_ref.1), custom_call_target="tpu_custom_call" | custom-call | tf_op jit(solution)/shard_map/pallas_call | solution.py:121
  2.0 35.4 %all_to_all.30.clips_ref = bf16[16,64,512]{2,1,0:T(8,128)(2,1)S(1)} all-to-all(bf16[16,64,512]{2,1,0:T(8,128)(2,1)S(1)} %shard_map.49), channel_id=1, replica_groups=mesh['z'=2,'q'=4,'p'=2,'h'=4,'x'=4,'c'=2] {'z','q','p'}, dimensions={0} | all-to-all | bytes 2097152 | tf_op jit(solution)/shard_map/all_to_all | solution.py:71
  37.4 0.6 shard_map.50
  38.0 1.9 %collective-permute-start = (f32[512,256]{1,0:T(8,128)S(1)}, f32[512,256]{1,0:T(8,128)S(1)}, u32[]{:S(2)}, u32[]{:S(2)}) collective-permute-start(f32[512,256]{1,0:T(8,128)S(1)} %get-tuple-element.15), channel_id=1, source_target_pairs={{0,1},{1,0},{2,3},{3,2},{4,5},{5,4},{6,7},{7,6},{8,9},{9,8},{10,11... | collective-permute-start | bytes 1572872 | tf_op jit(solution)/shard_map/ppermute | solution.py:143
  39.9 1.9 %collective-permute-done = f32[512,256]{1,0:T(8,128)S(1)} collective-permute-done((f32[512,256]{1,0:T(8,128)S(1)}, f32[512,256]{1,0:T(8,128)S(1)}, u32[]{:S(2)}, u32[]{:S(2)}) %collective-permute-start) | collective-permute-done | bytes 524320 | tf_op jit(solution)/shard_map/ppermute | solution.py:143
  41.8 0.1 add.11
  41.8 16.1 %all_to_all.31.parts_ref = f32[16,32,256]{2,1,0:T(8,128)S(1)} all-to-all(f32[16,32,256]{2,1,0:T(8,128)S(1)} %bitcast.11), channel_id=1, replica_groups=mesh['z'=2,'q'=4,'p'=2,'h'=4,'x'=4,'c'=2] {'x','z','p'}, dimensions={0} | all-to-all | bytes 1048576 | tf_op jit(solution)/shard_map/all_to_all | solution.py:71
  57.9 18.1 %all_to_all.32.parts_ref = f32[4,32,256]{2,1,0:T(8,128)S(1)} all-to-all(f32[4,32,256]{2,1,0:T(8,128)S(1)} %shard_map.51), channel_id=1, replica_groups=mesh['z'=2,'q'=4,'p'=2,'h'=4,'x'=4,'c'=2] {'h'}, dimensions={0} | all-to-all | bytes 262144 | tf_op jit(solution)/shard_map/all_to_all | solution.py:71
  76.1 11.8 %all_to_all.33.parts_ref = f32[4,32,256]{2,1,0:T(8,128)S(1)} all-to-all(f32[4,32,256]{2,1,0:T(8,128)S(1)} %shard_map.52), channel_id=1, replica_groups=mesh['z'=2,'q'=4,'p'=2,'h'=4,'x'=4,'c'=2] {'q'}, dimensions={0} | all-to-all | bytes 262144 | tf_op jit(solution)/shard_map/all_to_all | solution.py:71
  88.0 11.9 %all_to_all.34 = f32[16,32,256]{2,1,0:T(8,128)S(1)} all-to-all(f32[16,32,256]{2,1,0:T(8,128)S(1)} %shard_map.53), channel_id=1, replica_groups=mesh['z'=2,'q'=4,'p'=2,'h'=4,'x'=4,'c'=2] {'x','z','p'}, dimensions={0} | all-to-all | bytes 1048576 | tf_op jit(solution)/shard_map/all_to_all | solution.py:71
  99.9 1.9 %collective-permute-start.1 = (f32[512,256]{1,0:T(8,128)S(1)}, f32[512,256]{1,0:T(8,128)S(1)}, u32[]{:S(2)}, u32[]{:S(2)}) collective-permute-start(f32[512,256]{1,0:T(8,128)S(1)} %bitcast.8), channel_id=1, source_target_pairs={{0,1},{1,0},{2,3},{3,2},{4,5},{5,4},{6,7},{7,6},{8,9},{9,8},{10,11... | collective-permute-start | bytes 1572872 | tf_op jit(solution)/shard_map/ppermute | solution.py:149
  101.8 1.9 %collective-permute-done.1.other_ref = f32[512,256]{1,0:T(8,128)S(1)} collective-permute-done((f32[512,256]{1,0:T(8,128)S(1)}, f32[512,256]{1,0:T(8,128)S(1)}, u32[]{:S(2)}, u32[]{:S(2)}) %collective-permute-start.1) | collective-permute-done | bytes 524320 | tf_op jit(solution)/shard_map/ppermute | solution.py:149
  103.7 3.2 %shard_map.54 = (bf16[2,256,512]{2,1,0:T(8,128)(2,1)S(1)}, f32[1,512]{1,0:T(1,128)}, f32[1,32]{1,0:T(1,128)}) custom-call(s32[1]{0:T(128)} %bitcast.core_ref, s32[1]{0:T(128)} %bitcast.1.group_ref, f32[512,256]{1,0:T(8,128)S(1)} %bitcast.9, f32[512,256]{1,0:T(8,128)S(1)} %collective-permute-done.1.other_ref, bf16[16,64,512]{2,1,0:T(8,128)(2,1)S(1)} %all_to_all.30.clips_ref), custom_call_target="tpu_custom_call" | custom-call | tf_op jit(solution)/shard_map/pallas_call | solution.py:151
  106.9 19.3 %all_to_all.35 = bf16[16,32,512]{2,1,0:T(8,128)(2,1)S(1)} all-to-all(bf16[16,32,512]{2,1,0:T(8,128)(2,1)S(1)} %bitcast.10), channel_id=1, replica_groups=mesh['z'=2,'q'=4,'p'=2,'h'=4,'x'=4,'c'=2] {'z','q','p'}, dimensions={0} | all-to-all | bytes 1048576 | tf_op jit(solution)/shard_map/all_to_all | solution.py:71
  126.2 1.1 copy.6
  (3 shorter events, 0.1 us)
Async XLA Ops:
  38.0 3.8 %collective-permute-start = (f32[512,256]{1,0:T(8,128)S(1)}, f32[512,256]{1,0:T(8,128)S(1)}, u32[]{:S(2)}, u32[]{:S(2)}) collective-permute-start(f32[512,256]{1,0:T(8,128)S(1)} %get-tuple-element.15), channel_id=1, source_target_pairs={{0,1},{1,0},{2,3},{3,2},{4,5},{5,4},{6,7},{7,6},{8,9},{9,8},{10,11... | collective-permute-start | bytes 1572872 | tf_op jit(solution)/shard_map/ppermute | solution.py:143
  99.9 3.8 %collective-permute-start.1 = (f32[512,256]{1,0:T(8,128)S(1)}, f32[512,256]{1,0:T(8,128)S(1)}, u32[]{:S(2)}, u32[]{:S(2)}) collective-permute-start(f32[512,256]{1,0:T(8,128)S(1)} %bitcast.8), channel_id=1, source_target_pairs={{0,1},{1,0},{2,3},{3,2},{4,5},{5,4},{6,7},{7,6},{8,9},{9,8},{10,11... | collective-permute-start | bytes 1572872 | tf_op jit(solution)/shard_map/ppermute | solution.py:149

commit v6 on v5

v6 whole, which is shorter than its diff:
```python
import functools
import math

import jax
import jax.numpy as jnp
from jax import lax
from jax.experimental import pallas as pl
from jax.experimental.pallas import tpu as pltpu
from jax.sharding import Mesh, PartitionSpec as P

ITERS = 4
BLUR = 0.5
FINE = {"z": 2, "q": 4, "p": 2, "h": 4, "x": 4, "c": 2}
DP = ("z", "q", "p")
SEQ = ("h", "x", "c")
NEAR = ("x", "z", "p")
ANY = pl.BlockSpec(memory_space=pl.ANY)
HBM = pl.BlockSpec(memory_space=pltpu.HBM)
VMEM = pl.BlockSpec(memory_space=pltpu.VMEM)
SMEM = pl.BlockSpec(memory_space=pltpu.SMEM)
LIMIT = pltpu.CompilerParams(vmem_limit_bytes=32 * 1024 * 1024)


def pack_kernel(noise_ref, latents_ref, out_ref, held, arrived):
    local = noise_ref.shape[0]
    copies = [
        pltpu.make_async_copy(given, held.at[k], arrived.at[k])
        for k, given in enumerate((noise_ref, latents_ref))
    ]
    for copy in copies:
        copy.start()
    for k, copy in enumerate(copies):
        copy.wait()
        out_ref[:, k * local : (k + 1) * local, :] = jnp.swapaxes(held[k], 0, 1)


def pair_kernel(factor, clips_ref, out_ref):
    sources, both, width = clips_ref.shape
    local = both // 2
    noise = clips_ref[:, :local, :].reshape(sources * local, width)
    latents = clips_ref[:, local:, :].reshape(sources * local, width)
    wide = noise.astype(jnp.float32)
    noise_norms = jnp.sum(wide * wide, axis=1, keepdims=True) * factor
    wide = latents.astype(jnp.float32)
    latent_norms = jnp.sum(wide * wide, axis=1, keepdims=True) * factor
    latent_norms = jnp.transpose(jnp.broadcast_to(latent_norms, (sources * local, 128)))[:1, :]
    cross = lax.dot_general(
        noise, latents, (((1,), (1,)), ((), ())), preferred_element_type=jnp.float32
    )
    out_ref[...] = noise_norms + latent_norms - (2.0 * factor) * cross


def spread_kernel(parts_ref, out_ref):
    out_ref[...] = jnp.broadcast_to(jnp.sum(parts_ref[...], axis=0)[None], out_ref.shape)


def spread(parts, copies):
    return pl.pallas_call(
        spread_kernel,
        out_shape=jax.ShapeDtypeStruct((copies, *parts.shape[1:]), parts.dtype),
        in_specs=[VMEM],
        out_specs=VMEM,
        compiler_params=LIMIT,
    )(parts)


def exchange(blocks, axes):
    return lax.all_to_all(blocks, axes, 0, 0, tiled=True)


def weigh(group, local, scores, row_ref, column_ref):
    total = scores.shape[0]
    log_mass = -math.log2(total)
    row = jnp.zeros((total, 1), jnp.float32)
    for step in range(ITERS):
        value = row - scores[...]
        top = jnp.max(value, axis=0, keepdims=True)
        mass = jnp.sum(jnp.exp2(value - top), axis=0, keepdims=True)
        column = log_mass - (top + jnp.log2(mass))
        value = column - scores[...]
        top = jnp.max(value, axis=1, keepdims=True)
        mass = jnp.sum(jnp.exp2(value - top), axis=1, keepdims=True)
        row = log_mass - (top + jnp.log2(mass))
    back = BLUR * math.log(2.0)
    row_ref[...] = jnp.transpose(jnp.broadcast_to(row * back, (total, 128)))[:1, :]
    placed = pltpu.roll(column * back, lax.rem(total - group * local, total), 1)
    column_ref[...] = placed[:, :local]
    plan = jnp.exp2((row + column) - scores[...])
    return (plan * (1.0 / jnp.sum(plan, axis=0, keepdims=True))).astype(jnp.bfloat16)


def far_kernel(group_ref, scores, clips_ref, moved_ref, row_ref, column_ref):
    sources, both, width = clips_ref.shape
    local = both // 2
    weights = weigh(group_ref[0], local, scores, row_ref, column_ref)
    noise = clips_ref[:, :local, :].reshape(sources * local, width)
    moved = lax.dot_general(
        weights, noise, (((0,), (0,)), ((), ())), preferred_element_type=jnp.float32
    )
    moved_ref[...] = moved.astype(jnp.bfloat16).reshape(moved_ref.shape)


def blank_kernel(out_ref):
    pass


def blank(shape, dtype):
    return pl.pallas_call(
        blank_kernel, out_shape=jax.ShapeDtypeStruct(shape, dtype), out_specs=ANY
    )()


def per_device(latents, noise):
    local, channels, width = latents.shape
    dp, seq, near = lax.axis_size(DP), lax.axis_size(SEQ), lax.axis_size(NEAR)
    total = local * dp
    factor = math.log2(math.e) / (BLUR * math.sqrt(channels * width * seq))
    group = lax.axis_index(DP).reshape(1).astype(jnp.int32)

    packed = pl.pallas_call(
        pack_kernel,
        out_shape=jax.ShapeDtypeStruct((channels, 2 * local, width), noise.dtype),
        in_specs=[HBM, HBM],
        out_specs=VMEM,
        scratch_shapes=[
            pltpu.VMEM((2, *noise.shape), noise.dtype),
            pltpu.SemaphoreType.DMA((2,)),
        ],
        compiler_params=LIMIT,
    )(*(pltpu.with_memory_space_constraint(given, pltpu.HBM) for given in (noise, latents)))
    packed, group = lax.optimization_barrier((packed, group))
    clips = exchange(packed, DP)

    terms = pl.pallas_call(
        functools.partial(pair_kernel, factor),
        out_shape=jax.ShapeDtypeStruct((total, total), jnp.float32),
        in_specs=[VMEM],
        out_specs=VMEM,
        compiler_params=LIMIT,
    )(clips)
    summed = terms + lax.ppermute(terms, "c", [(0, 1)])

    def reduce_cost(summed):
        parts = exchange(summed.reshape(near, total // near, total), NEAR)
        parts = exchange(spread(parts, lax.axis_size("h")), "h")
        parts = exchange(spread(parts, lax.axis_size("q")), "q")
        return exchange(spread(parts, near), NEAR).reshape(total, total)

    def move(cost, clips, group):
        moved, row, column = pl.pallas_call(
            far_kernel,
            out_shape=(jax.ShapeDtypeStruct((dp, local, width), noise.dtype), *ends),
            in_specs=[SMEM, VMEM, VMEM],
            out_specs=(VMEM, VMEM, VMEM),
            compiler_params=LIMIT,
        )(group, cost, clips)
        return exchange(moved, DP), row, column

    ends = (jax.ShapeDtypeStruct((1, total), jnp.float32), jax.ShapeDtypeStruct((1, local), jnp.float32))
    upper = lax.axis_index("c") == 1
    cost = lax.cond(upper, reduce_cost, lambda summed: blank((total, total), jnp.float32), summed)
    sent = lax.ppermute(cost, "c", [(1, 0)])
    done = lax.cond(
        upper,
        move,
        lambda cost, clips, group: (blank((dp, local, width), noise.dtype), *(blank(e.shape, e.dtype) for e in ends)),
        cost, clips, group,
    )
    targets, row, column = lax.cond(
        upper, lambda done, sent, clips, group: done, lambda done, sent, clips, group: move(sent, clips, group), done, sent, clips, group
    )
    return (targets.swapaxes(0, 1), row.reshape(total), column.reshape(local))


def solution(mesh):
    fine = Mesh(mesh.devices.reshape(tuple(FINE.values())), tuple(FINE))
    in_specs = (P(DP, None, SEQ), P(DP, None, SEQ))
    out_specs = (P(DP, None, SEQ), P(), P(DP))
    return jax.shard_map(
        per_device, mesh=fine, in_specs=in_specs, out_specs=out_specs, check_vma=False
    )
```

time: 128 us -> 127 us (level)
  waiting for transfers between devices: 3.75 us -> 63.7 us
  blocking collectives: 113 us -> 53.5 us
    ppermute x2, waiting for transfers between devices: 3.75 us -> 63.7 us  [the longest x1 61.5 us: per_device(): sent = lax.ppermute(cost, 'c', [(1, 0)])]
    all_to_all x6 -> x2, blocking collectives: 113 us -> 53.5 us  [exchange(): return lax.all_to_all(blocks, axes, 0, 0, tiled=True)]
    pallas_call x5 -> x6, Pallas kernels: 3.85 us -> 3.59 us  [the longest x1 3.05 us: move(): pl.pallas_call(far_kernel, out_shape=(jax.ShapeDtypeStruct((dp, local, wi...]
where the time goes in v6:
time: 127 us
  waiting for transfers between devices  63.7 us (50%)
  blocking collectives  53.5 us (42%)
  Pallas kernels  4.94 us (4%)
  starting transfers between devices  2.64 us (2%)
    ppermute x1, waiting for transfers between devices, per_device(): sent = lax.ppermute(cost, 'c', [(1, 0)])  61.5 us
    all_to_all x2, blocking collectives, exchange(): return lax.all_to_all(blocks, axes, 0, 0, tiled=True)  53.5 us
    pallas_call x1, Pallas kernels, move(): pl.pallas_call(far_kernel, out_shape=(jax.ShapeDtypeStruct((dp, local, wi...  3.05 us
  transfers between devices with their start and end apart: 2, of which 2 were waited for; matrix products, arithmetic and copies ran while one was open for 0% of the time, Pallas kernels for 0%

profile of v6, /device:TPU:8, one launch (start us, length us, event | category | flops | bytes accessed | tf_op | source)
XLA Modules:
  0.0 126.6 jit_solution(5814533301249131420)
XLA Ops:
  0.6 1.3 %shard_map.49 = bf16[16,64,512]{2,1,0:T(8,128)(2,1)S(1)} custom-call(bf16[32,16,512]{2,1,0:T(8,128)(2,1)} %noise_ref.1, bf16[32,16,512]{2,1,0:T(8,128)(2,1)} %latents_ref.1), custom_call_target="tpu_custom_call" | custom-call | tf_op jit(solution)/shard_map/pallas_call | solution.py:120
  2.0 35.4 %all_to_all.35.clips_ref = bf16[16,64,512]{2,1,0:T(8,128)(2,1)S(1)} all-to-all(bf16[16,64,512]{2,1,0:T(8,128)(2,1)S(1)} %shard_map.49), channel_id=1, replica_groups=mesh['z'=2,'q'=4,'p'=2,'h'=4,'x'=4,'c'=2] {'z','q','p'}, dimensions={0} | all-to-all | bytes 2097152 | tf_op jit(solution)/shard_map/all_to_all | solution.py:68
  37.4 0.5 shard_map.50
  37.9 1.4 %collective-permute-start = (f32[512,512]{1,0:T(8,128)S(1)}, f32[512,512]{1,0:T(8,128)S(1)}, u32[]{:S(2)}, u32[]{:S(2)}) collective-permute-start(f32[512,512]{1,0:T(8,128)S(1)} %shard_map.50), channel_id=1, source_target_pairs={{0,1},{2,3},{4,5},{6,7},{8,9},{10,11},{12,13},{14,15},{16,17},{18,... | collective-permute-start | bytes 3145736 | tf_op jit(solution)/shard_map/ppermute | solution.py:141
  39.3 2.2 %collective-permute-done = f32[512,512]{1,0:T(8,128)S(1)} collective-permute-done((f32[512,512]{1,0:T(8,128)S(1)}, f32[512,512]{1,0:T(8,128)S(1)}, u32[]{:S(2)}, u32[]{:S(2)}) %collective-permute-start) | collective-permute-done | bytes 1048608 | tf_op jit(solution)/shard_map/ppermute | solution.py:141
  41.5 1.3 %collective-permute-start.1 = (f32[512,512]{1,0:T(8,128)}, f32[512,512]{1,0:T(8,128)S(1)}, u32[]{:S(2)}, u32[]{:S(2)}) collective-permute-start(f32[512,512]{1,0:T(8,128)} %get-tuple-element.65), channel_id=1, source_target_pairs={{1,0},{3,2},{5,4},{7,6},{9,8},{11,10},{13,12},{15,14},{17,16},{19,... | collective-permute-start | bytes 3145736 | tf_op jit(solution)/shard_map/ppermute | solution.py:162
  42.8 61.5 %collective-permute-done.1 = f32[512,512]{1,0:T(8,128)S(1)} collective-permute-done((f32[512,512]{1,0:T(8,128)}, f32[512,512]{1,0:T(8,128)S(1)}, u32[]{:S(2)}, u32[]{:S(2)}) %collective-permute-start.1) | collective-permute-done | bytes 1048608 | tf_op jit(solution)/shard_map/ppermute | solution.py:162
  104.4 21.2 %conditional.5 = ((bf16[16,32,512]{2,1,0:T(8,128)(2,1)S(1)}, f32[1,512]{1,0:T(1,128)}, f32[1,32]{1,0:T(1,128)})) conditional(s32[]{:T(128)} %convert_element_type.2, (s32[1]{0:T(128)}, f32[512,512]{1,0:T(8,128)S(1)}, bf16[16,64,512]{2,1,0:T(8,128)(2,1)S(1)}) %tuple.33, (bf16[16,32,512]{2,1,0:T(8,128)(2,1)S(1)}, f32[1,512]{1,0:T(1,128)}, ...), branch_computations={%region_4.0_spmd, %region_5.0_spmd} | conditional | bytes 1048608 | solution.py:169
  104.4 3.1 %branch_0_fun.9 = (bf16[16,32,512]{2,1,0:T(8,128)(2,1)S(1)}, f32[1,512]{1,0:T(1,128)}, f32[1,32]{1,0:T(1,128)}) custom-call(s32[1]{0:T(128)} %get-tuple-element.34.group_ref, f32[512,512]{1,0:T(8,128)S(1)} %get-tuple-element.35.scores, bf16[16,64,512]{2,1,0:T(8,128)(2,1)S(1)} %get-tuple-element.36.clips_ref), custom_call_target="tpu_custom_call" | custom-call | tf_op jit(solution)/shard_map/cond/branch_0_fun/pallas_call | solution.py:150
  107.4 18.1 %all_to_all.34 = bf16[16,32,512]{2,1,0:T(8,128)(2,1)S(1)} all-to-all(bf16[16,32,512]{2,1,0:T(8,128)(2,1)S(1)} %get-tuple-element.37), channel_id=1, replica_groups=mesh['z'=2,'q'=4,'p'=2,'h'=4,'x'=4,'c'=2] {'z','q','p'}, dimensions={0} | all-to-all | bytes 1048576 | tf_op jit(solution)/shard_map/cond/branch_0_fun/all_to_all | solution.py:68
  125.5 1.1 copy.7
  (6 shorter events, 0.0 us)
Async XLA Ops:
  37.9 3.6 %collective-permute-start = (f32[512,512]{1,0:T(8,128)S(1)}, f32[512,512]{1,0:T(8,128)S(1)}, u32[]{:S(2)}, u32[]{:S(2)}) collective-permute-start(f32[512,512]{1,0:T(8,128)S(1)} %shard_map.50), channel_id=1, source_target_pairs={{0,1},{2,3},{4,5},{6,7},{8,9},{10,11},{12,13},{14,15},{16,17},{18,... | collective-permute-start | bytes 3145736 | tf_op jit(solution)/shard_map/ppermute | solution.py:141
  41.5 62.9 %collective-permute-start.1 = (f32[512,512]{1,0:T(8,128)}, f32[512,512]{1,0:T(8,128)S(1)}, u32[]{:S(2)}, u32[]{:S(2)}) collective-permute-start(f32[512,512]{1,0:T(8,128)} %get-tuple-element.65), channel_id=1, source_target_pairs={{1,0},{3,2},{5,4},{7,6},{9,8},{11,10},{13,12},{15,14},{17,16},{19,... | collective-permute-start | bytes 3145736 | tf_op jit(solution)/shard_map/ppermute | solution.py:162

commit v7 on v6

--- a/solution.py
+++ b/solution.py
@@ -21,7 +21,8 @@
 LIMIT = pltpu.CompilerParams(vmem_limit_bytes=32 * 1024 * 1024)
 
 
-def pack_kernel(noise_ref, latents_ref, out_ref, held, arrived):
+def pack_kernel(noise_ref, latents_ref, *rest):
+    *out_refs, held, arrived = rest
     local = noise_ref.shape[0]
     copies = [
         pltpu.make_async_copy(given, held.at[k], arrived.at[k])
@@ -31,23 +32,54 @@
         copy.start()
     for k, copy in enumerate(copies):
         copy.wait()
-        out_ref[:, k * local : (k + 1) * local, :] = jnp.swapaxes(held[k], 0, 1)
-
-
-def pair_kernel(factor, clips_ref, out_ref):
-    sources, both, width = clips_ref.shape
-    local = both // 2
-    noise = clips_ref[:, :local, :].reshape(sources * local, width)
-    latents = clips_ref[:, local:, :].reshape(sources * local, width)
+        turned = jnp.swapaxes(held[k], 0, 1)
+        first = 0
+        for out_ref in out_refs:
+            last = first + out_ref.shape[1]
+            low, high = max(first, k * local), min(last, (k + 1) * local)
+            if low < high:
+                out_ref[:, low - first : high - first, :] = turned[:, low - k * local : high - k * local, :]
+            first = last
+
+
+def pack(noise, latents, runs):
+    local, channels, width = noise.shape
+    return pl.pallas_call(
+        pack_kernel,
+        out_shape=tuple(jax.ShapeDtypeStruct((channels, rows, width), noise.dtype) for rows in runs),
+        in_specs=[HBM, HBM],
+        out_specs=(VMEM,) * len(runs),
+        scratch_shapes=[
+            pltpu.VMEM((2, *noise.shape), noise.dtype),
+            pltpu.SemaphoreType.DMA((2,)),
+        ],
+        compiler_params=LIMIT,
+    )(*(pltpu.with_memory_space_constraint(given, pltpu.HBM) for given in (noise, latents)))
+
+
+def noise_of(local, head_ref, rest_ref):
+    sources, head, width = head_ref.shape
+    noise = jnp.concatenate([head_ref[...], rest_ref[:, : local - head, :]], axis=1)
+    return noise.reshape(sources * local, width)
+
+
+def pair_kernel(factor, head_ref, rest_ref, out_ref, *tail_refs):
+    sources, head, width = head_ref.shape
+    local = (head + rest_ref.shape[1]) // 2
+    total = sources * local
+    noise = noise_of(local, head_ref, rest_ref)
+    latents = rest_ref[:, local - head :, :].reshape(total, width)
     wide = noise.astype(jnp.float32)
     noise_norms = jnp.sum(wide * wide, axis=1, keepdims=True) * factor
     wide = latents.astype(jnp.float32)
     latent_norms = jnp.sum(wide * wide, axis=1, keepdims=True) * factor
-    latent_norms = jnp.transpose(jnp.broadcast_to(latent_norms, (sources * local, 128)))[:1, :]
+    latent_norms = jnp.transpose(jnp.broadcast_to(latent_norms, (total, 128)))[:1, :]
     cross = lax.dot_general(
         noise, latents, (((1,), (1,)), ((), ())), preferred_element_type=jnp.float32
     )
     out_ref[...] = noise_norms + latent_norms - (2.0 * factor) * cross
+    for tail_ref in tail_refs:
+        tail_ref[...] = rest_ref[:, : local - head, :]
 
 
 def spread_kernel(parts_ref, out_ref):
@@ -89,11 +121,10 @@
     return (plan * (1.0 / jnp.sum(plan, axis=0, keepdims=True))).astype(jnp.bfloat16)
 
 
-def far_kernel(group_ref, scores, clips_ref, moved_ref, row_ref, column_ref):
-    sources, both, width = clips_ref.shape
-    local = both // 2
+def coupling_kernel(group_ref, scores, head_ref, rest_ref, moved_ref, row_ref, column_ref):
+    local = column_ref.shape[1]
+    noise = noise_of(local, head_ref, rest_ref)
     weights = weigh(group_ref[0], local, scores, row_ref, column_ref)
-    noise = clips_ref[:, :local, :].reshape(sources * local, width)
     moved = lax.dot_general(
         weights, noise, (((0,), (0,)), ((), ())), preferred_element_type=jnp.float32
     )
@@ -117,30 +148,47 @@
     factor = math.log2(math.e) / (BLUR * math.sqrt(channels * width * seq))
     group = lax.axis_index(DP).reshape(1).astype(jnp.int32)
 
-    packed = pl.pallas_call(
-        pack_kernel,
-        out_shape=jax.ShapeDtypeStruct((channels, 2 * local, width), noise.dtype),
-        in_specs=[HBM, HBM],
-        out_specs=VMEM,
-        scratch_shapes=[
-            pltpu.VMEM((2, *noise.shape), noise.dtype),
-            pltpu.SemaphoreType.DMA((2,)),
-        ],
-        compiler_params=LIMIT,
-    )(*(pltpu.with_memory_space_constraint(given, pltpu.HBM) for given in (noise, latents)))
-    packed, group = lax.optimization_barrier((packed, group))
-    clips = exchange(packed, DP)
-
-    terms = pl.pallas_call(
-        functools.partial(pair_kernel, factor),
-        out_shape=jax.ShapeDtypeStruct((total, total), jnp.float32),
-        in_specs=[VMEM],
-        out_specs=VMEM,
-        compiler_params=LIMIT,
-    )(clips)
-    summed = terms + lax.ppermute(terms, "c", [(0, 1)])
-
-    def reduce_cost(summed):
+    head = local // 2
+    upper = lax.axis_index("c") == 1
+
+    square = (total, total)
+
+    tail = (dp, local - head, width)
+
+    def pair_terms(clips, tails=0):
+        return pl.pallas_call(
+            functools.partial(pair_kernel, factor),
+            out_shape=(jax.ShapeDtypeStruct(square, jnp.float32),)
+            + (jax.ShapeDtypeStruct(tail, noise.dtype),) * tails,
+            in_specs=[VMEM, VMEM],
+            out_specs=(VMEM,) * (1 + tails),
+            compiler_params=LIMIT,
+        )(*clips)
+
+    def start_upper(noise, latents):
+        first, second = pack(noise, latents, (head, 2 * local - head))
+        first, second, unused = lax.optimization_barrier((first, second, blank(square, jnp.float32)))
+        first, second = lax.optimization_barrier((exchange(first, DP), second))
+        return first, second, unused
+
+    def start_lower(noise, latents):
+        (packed,) = pack(noise, latents, (2 * local,))
+        clips = exchange(packed, DP)
+        clips = clips[:, :head], clips[:, head:]
+        return *clips, *pair_terms(clips)
+
+    def finish_upper(first, second):
+        return pair_terms((first, exchange(second, DP)), tails=1)
+
+    def finish_lower(first, second):
+        return blank(square, jnp.float32), blank(tail, noise.dtype)
+
+    first, second, terms = lax.cond(upper, start_upper, start_lower, noise, latents)
+    received = lax.ppermute(terms, "c", [(0, 1)])
+    upper_terms, upper_noise = lax.cond(upper, finish_upper, finish_lower, first, second)
+
+    def reduce_cost(terms, received):
+        summed = terms + received
         parts = exchange(summed.reshape(near, total // near, total), NEAR)
         parts = exchange(spread(parts, lax.axis_size("h")), "h")
         parts = exchange(spread(parts, lax.axis_size("q")), "q")
@@ -148,26 +196,35 @@
 
     def move(cost, clips, group):
         moved, row, column = pl.pallas_call(
-            far_kernel,
+            coupling_kernel,
             out_shape=(jax.ShapeDtypeStruct((dp, local, width), noise.dtype), *ends),
-            in_specs=[SMEM, VMEM, VMEM],
+            in_specs=[SMEM, VMEM, VMEM, VMEM],
             out_specs=(VMEM, VMEM, VMEM),
             compiler_params=LIMIT,
-        )(group, cost, clips)
+        )(group, cost, *clips)
         return exchange(moved, DP), row, column
 
     ends = (jax.ShapeDtypeStruct((1, total), jnp.float32), jax.ShapeDtypeStruct((1, local), jnp.float32))
-    upper = lax.axis_index("c") == 1
-    cost = lax.cond(upper, reduce_cost, lambda summed: blank((total, total), jnp.float32), summed)
+    cost = lax.cond(
+        upper, reduce_cost, lambda terms, received: blank(square, jnp.float32), upper_terms, received
+    )
     sent = lax.ppermute(cost, "c", [(1, 0)])
     done = lax.cond(
         upper,
         move,
         lambda cost, clips, group: (blank((dp, local, width), noise.dtype), *(blank(e.shape, e.dtype) for e in ends)),
-        cost, clips, group,
+        cost,
+        (first, upper_noise),
+        group,
     )
     targets, row, column = lax.cond(
-        upper, lambda done, sent, clips, group: done, lambda done, sent, clips, group: move(sent, clips, group), done, sent, clips, group
+        upper,
+        lambda done, sent, clips, group: done,
+        lambda done, sent, clips, group: move(sent, clips, group),
+        done,
+        sent,
+        (first, second),
+        group,
     )
     return (targets.swapaxes(0, 1), row.reshape(total), column.reshape(local))
 

time: 127 us -> 125 us (0.984)
  blocking collectives: 53.5 us -> 45.1 us
  waiting for transfers between devices: 63.7 us -> 69 us
    all_to_all x2, blocking collectives: 53.5 us -> 45.1 us  [exchange(): return lax.all_to_all(blocks, axes, 0, 0, tiled=True)]
    ppermute x1, waiting for transfers between devices: 61.5 us -> 66.7 us  [per_device(): sent = lax.ppermute(cost, 'c', [(1, 0)])]
where the time goes in v7:
time: 125 us
  waiting for transfers between devices  69 us (55%)
  blocking collectives  45.1 us (36%)
  Pallas kernels  5.93 us (5%)
  starting transfers between devices  2.62 us (2%)
    ppermute x1, waiting for transfers between devices, per_device(): sent = lax.ppermute(cost, 'c', [(1, 0)])  66.7 us
    all_to_all x2, blocking collectives, exchange(): return lax.all_to_all(blocks, axes, 0, 0, tiled=True)  45.1 us
    pallas_call x1, Pallas kernels, move(): pl.pallas_call(coupling_kernel, out_shape=(jax.ShapeDtypeStruct((dp, loca...  3.05 us
  transfers between devices with their start and end apart: 2, of which 2 were waited for; matrix products, arithmetic and copies ran while one was open for 0% of the time, Pallas kernels for 0%

profile of v7, /device:TPU:8, one launch (start us, length us, event | category | flops | bytes accessed | tf_op | source)
XLA Modules:
  0.0 124.6 jit_solution(10725089977959919316)
XLA Ops:
  0.6 29.9 %conditional.5 = (bf16[16,16,512]{2,1,0:T(8,128)(2,1)S(1)}, bf16[16,48,512]{2,1,0:T(8,128)(2,1)S(1)}, f32[512,512]{1,0:T(8,128)}) conditional(s32[]{:T(128)} %convert_element_type.2, (bf16[32,16,512]{2,1,0:T(8,128)(2,1)}, bf16[32,16,512]{2,1,0:T(8,128)(2,1)}) %tuple.47, (bf16[32,16,512]{2,1,0:T(8,128)(2,1)}, bf16[32,16,512]{2,1,0:T(8,128)(2,1)}) %tuple.47), branch_computations={%region_0.0_spmd, %region_1.0_spmd} | conditional | bytes 4194328 | solution.py:186
  0.6 1.3 %branch_0_fun.9 = bf16[16,64,512]{2,1,0:T(8,128)(2,1)S(1)} custom-call(bf16[32,16,512]{2,1,0:T(8,128)(2,1)} %get-tuple-element.38.noise_ref, bf16[32,16,512]{2,1,0:T(8,128)(2,1)} %get-tuple-element.42.latents_ref), custom_call_target="tpu_custom_call" | custom-call | tf_op jit(solution)/shard_map/cond/branch_0_fun/pallas_call | solution.py:47
  2.0 27.0 %all_to_all.36 = bf16[16,64,512]{2,1,0:T(8,128)(2,1)S(1)} all-to-all(bf16[16,64,512]{2,1,0:T(8,128)(2,1)S(1)} %branch_0_fun.9), channel_id=1, replica_groups=mesh['z'=2,'q'=4,'p'=2,'h'=4,'x'=4,'c'=2] {'z','q','p'}, dimensions={0} | all-to-all | bytes 2097152 | tf_op jit(solution)/shard_map/cond/branch_0_fun/all_to_all | solution.py:100
  29.0 0.1 slice.7.rest_ref
  29.0 1.5 %branch_0_fun.10 = f32[512,512]{1,0:T(8,128)} custom-call(bf16[16,16,512]{2,1,0:T(8,128)(2,1)S(1)} %slice.6.head_ref, bf16[16,48,512]{2,1,0:T(8,128)(2,1)S(1)} %slice.7.rest_ref), custom_call_target="tpu_custom_call" | custom-call | tf_op jit(solution)/shard_map/cond/branch_0_fun/pallas_call | solution.py:159
  30.6 1.3 %collective-permute-start = (f32[512,512]{1,0:T(8,128)}, f32[512,512]{1,0:T(8,128)S(1)}, u32[]{:S(2)}, u32[]{:S(2)}) collective-permute-start(f32[512,512]{1,0:T(8,128)} %get-tuple-element.84), channel_id=1, source_target_pairs={{0,1},{2,3},{4,5},{6,7},{8,9},{10,11},{12,13},{14,15},{16,17},{18,... | collective-permute-start | bytes 3145736 | tf_op jit(solution)/shard_map/ppermute | solution.py:187
  32.0 2.4 %collective-permute-done = f32[512,512]{1,0:T(8,128)S(1)} collective-permute-done((f32[512,512]{1,0:T(8,128)}, f32[512,512]{1,0:T(8,128)S(1)}, u32[]{:S(2)}, u32[]{:S(2)}) %collective-permute-start) | collective-permute-done | bytes 1048608 | tf_op jit(solution)/shard_map/ppermute | solution.py:187
  34.3 1.3 %collective-permute-start.1 = (f32[512,512]{1,0:T(8,128)}, f32[512,512]{1,0:T(8,128)S(1)}, u32[]{:S(2)}, u32[]{:S(2)}) collective-permute-start(f32[512,512]{1,0:T(8,128)} %get-tuple-element.112), channel_id=1, source_target_pairs={{1,0},{3,2},{5,4},{7,6},{9,8},{11,10},{13,12},{15,14},{17,16},{19,... | collective-permute-start | bytes 3145736 | tf_op jit(solution)/shard_map/ppermute | solution.py:211
  35.7 66.7 %collective-permute-done.1 = f32[512,512]{1,0:T(8,128)S(1)} collective-permute-done((f32[512,512]{1,0:T(8,128)}, f32[512,512]{1,0:T(8,128)S(1)}, u32[]{:S(2)}, u32[]{:S(2)}) %collective-permute-start.1) | collective-permute-done | bytes 1048608 | tf_op jit(solution)/shard_map/ppermute | solution.py:211
  102.4 21.2 %conditional.9 = ((bf16[16,32,512]{2,1,0:T(8,128)(2,1)S(1)}, f32[1,512]{1,0:T(1,128)}, f32[1,32]{1,0:T(1,128)})) conditional(s32[]{:T(128)} %convert_element_type.2, (s32[1]{0:T(128)}, f32[512,512]{1,0:T(8,128)S(1)}, bf16[16,16,512]{2,1,0:T(8,128)(2,1)S(1)}, bf16[16,48,512]{2,1,0:T(8,128)(2,1)S(1)}) %tuple.50, (bf16[16,32,512]{2,1,0:T(8,128)(2,1)S(1)}, ...), branch_computations={%region_8.0_spmd, %region_9.0_spmd} | conditional | bytes 1048608 | solution.py:220
  102.4 3.0 %branch_0_fun.17 = (bf16[16,32,512]{2,1,0:T(8,128)(2,1)S(1)}, f32[1,512]{1,0:T(1,128)}, f32[1,32]{1,0:T(1,128)}) custom-call(s32[1]{0:T(128)} %get-tuple-element.63.group_ref, f32[512,512]{1,0:T(8,128)S(1)} %get-tuple-element.64.scores, bf16[16,16,512]{2,1,0:T(8,128)(2,1)S(1)} %get-tuple-element.65.head_ref, bf16[16,48,512]{2,1,0:T(8,128)(2,1)S(1)} %get-tuple-element.66.rest_ref), custom_call_target="tpu_custom_call" | custom-call | tf_op jit(solution)/shard_map/cond/branch_0_fun/pallas_call | solution.py:198
  105.4 18.1 %all_to_all.44 = bf16[16,32,512]{2,1,0:T(8,128)(2,1)S(1)} all-to-all(bf16[16,32,512]{2,1,0:T(8,128)(2,1)S(1)} %get-tuple-element.67), channel_id=1, replica_groups=mesh['z'=2,'q'=4,'p'=2,'h'=4,'x'=4,'c'=2] {'z','q','p'}, dimensions={0} | all-to-all | bytes 1048576 | tf_op jit(solution)/shard_map/cond/branch_0_fun/all_to_all | solution.py:100
  123.6 1.1 copy.7
  (10 shorter events, 0.1 us)
Async XLA Ops:
  30.6 3.8 %collective-permute-start = (f32[512,512]{1,0:T(8,128)}, f32[512,512]{1,0:T(8,128)S(1)}, u32[]{:S(2)}, u32[]{:S(2)}) collective-permute-start(f32[512,512]{1,0:T(8,128)} %get-tuple-element.84), channel_id=1, source_target_pairs={{0,1},{2,3},{4,5},{6,7},{8,9},{10,11},{12,13},{14,15},{16,17},{18,... | collective-permute-start | bytes 3145736 | tf_op jit(solution)/shard_map/ppermute | solution.py:187
  34.3 68.0 %collective-permute-start.1 = (f32[512,512]{1,0:T(8,128)}, f32[512,512]{1,0:T(8,128)S(1)}, u32[]{:S(2)}, u32[]{:S(2)}) collective-permute-start(f32[512,512]{1,0:T(8,128)} %get-tuple-element.112), channel_id=1, source_target_pairs={{1,0},{3,2},{5,4},{7,6},{9,8},{11,10},{13,12},{15,14},{17,16},{19,... | collective-permute-start | bytes 3145736 | tf_op jit(solution)/shard_map/ppermute | solution.py:211

commit v8 on v7

--- a/solution.py
+++ b/solution.py
@@ -9,6 +9,7 @@
 from jax.sharding import Mesh, PartitionSpec as P
 
 ITERS = 4
+PARTS = 2
 BLUR = 0.5
 FINE = {"z": 2, "q": 4, "p": 2, "h": 4, "x": 4, "c": 2}
 DP = ("z", "q", "p")
@@ -23,7 +24,8 @@
 
 def pack_kernel(noise_ref, latents_ref, *rest):
     *out_refs, held, arrived = rest
-    local = noise_ref.shape[0]
+    local, _, width = noise_ref.shape
+    width //= PARTS
     copies = [
         pltpu.make_async_copy(given, held.at[k], arrived.at[k])
         for k, given in enumerate((noise_ref, latents_ref))
@@ -33,20 +35,23 @@
     for k, copy in enumerate(copies):
         copy.wait()
         turned = jnp.swapaxes(held[k], 0, 1)
-        first = 0
-        for out_ref in out_refs:
-            last = first + out_ref.shape[1]
-            low, high = max(first, k * local), min(last, (k + 1) * local)
-            if low < high:
-                out_ref[:, low - first : high - first, :] = turned[:, low - k * local : high - k * local, :]
-            first = last
+        for part in range(PARTS):
+            start = (part * 2 + k) * local
+            piece = turned[:, :, part * width : (part + 1) * width]
+            first = 0
+            for out_ref in out_refs:
+                last = first + out_ref.shape[1]
+                low, high = max(first, start), min(last, start + local)
+                if low < high:
+                    out_ref[:, low - first : high - first, :] = piece[:, low - start : high - start, :]
+                first = last
 
 
 def pack(noise, latents, runs):
     local, channels, width = noise.shape
     return pl.pallas_call(
         pack_kernel,
-        out_shape=tuple(jax.ShapeDtypeStruct((channels, rows, width), noise.dtype) for rows in runs),
+        out_shape=tuple(jax.ShapeDtypeStruct((channels, rows, width // PARTS), noise.dtype) for rows in runs),
         in_specs=[HBM, HBM],
         out_specs=(VMEM,) * len(runs),
         scratch_shapes=[
@@ -57,29 +62,37 @@
     )(*(pltpu.with_memory_space_constraint(given, pltpu.HBM) for given in (noise, latents)))
 
 
-def noise_of(local, head_ref, rest_ref):
+def noise_of(head_ref, rest_ref, local, skipped):
     sources, head, width = head_ref.shape
-    noise = jnp.concatenate([head_ref[...], rest_ref[:, : local - head, :]], axis=1)
-    return noise.reshape(sources * local, width)
+    tail = local - head
+    first = jnp.concatenate([head_ref[...], rest_ref[:, :tail, :]], axis=1)
+    second = rest_ref[:, tail + skipped : tail + skipped + local, :]
+    return [noise.reshape(sources * local, width) for noise in (first, second)]
 
 
 def pair_kernel(factor, head_ref, rest_ref, out_ref, *tail_refs):
     sources, head, width = head_ref.shape
-    local = (head + rest_ref.shape[1]) // 2
+    local = (head + rest_ref.shape[1]) // (2 * PARTS)
     total = sources * local
-    noise = noise_of(local, head_ref, rest_ref)
-    latents = rest_ref[:, local - head :, :].reshape(total, width)
-    wide = noise.astype(jnp.float32)
-    noise_norms = jnp.sum(wide * wide, axis=1, keepdims=True) * factor
-    wide = latents.astype(jnp.float32)
-    latent_norms = jnp.sum(wide * wide, axis=1, keepdims=True) * factor
-    latent_norms = jnp.transpose(jnp.broadcast_to(latent_norms, (total, 128)))[:1, :]
-    cross = lax.dot_general(
-        noise, latents, (((1,), (1,)), ((), ())), preferred_element_type=jnp.float32
-    )
-    out_ref[...] = noise_norms + latent_norms - (2.0 * factor) * cross
+    tail = local - head
+    noises = noise_of(head_ref, rest_ref, local, local)
+    terms = 0.0
+    for part, noise in enumerate(noises):
+        first = tail + 2 * part * local
+        latents = rest_ref[:, first : first + local, :].reshape(total, width)
+        wide = noise.astype(jnp.float32)
+        noise_norms = jnp.sum(wide * wide, axis=1, keepdims=True) * factor
+        wide = latents.astype(jnp.float32)
+        latent_norms = jnp.sum(wide * wide, axis=1, keepdims=True) * factor
+        latent_norms = jnp.transpose(jnp.broadcast_to(latent_norms, (total, 128)))[:1, :]
+        cross = lax.dot_general(
+            noise, latents, (((1,), (1,)), ((), ())), preferred_element_type=jnp.float32
+        )
+        terms += noise_norms + latent_norms - (2.0 * factor) * cross
+    out_ref[...] = terms
     for tail_ref in tail_refs:
-        tail_ref[...] = rest_ref[:, : local - head, :]
+        tail_ref[:, :tail, :] = rest_ref[:, :tail, :]
+        tail_ref[:, tail:, :] = rest_ref[:, tail + local : tail + 2 * local, :]
 
 
 def spread_kernel(parts_ref, out_ref):
@@ -121,14 +134,16 @@
     return (plan * (1.0 / jnp.sum(plan, axis=0, keepdims=True))).astype(jnp.bfloat16)
 
 
-def coupling_kernel(group_ref, scores, head_ref, rest_ref, moved_ref, row_ref, column_ref):
+def coupling_kernel(skipped, group_ref, scores, head_ref, rest_ref, moved_ref, row_ref, column_ref):
     local = column_ref.shape[1]
-    noise = noise_of(local, head_ref, rest_ref)
+    width = head_ref.shape[2]
     weights = weigh(group_ref[0], local, scores, row_ref, column_ref)
-    moved = lax.dot_general(
-        weights, noise, (((0,), (0,)), ((), ())), preferred_element_type=jnp.float32
-    )
-    moved_ref[...] = moved.astype(jnp.bfloat16).reshape(moved_ref.shape)
+    for part, noise in enumerate(noise_of(head_ref, rest_ref, local, skipped)):
+        moved = lax.dot_general(
+            weights, noise, (((0,), (0,)), ((), ())), preferred_element_type=jnp.float32
+        )
+        moved = moved.astype(jnp.bfloat16).reshape(-1, local, width)
+        moved_ref[:, :, part * width : (part + 1) * width] = moved
 
 
 def blank_kernel(out_ref):
@@ -153,7 +168,7 @@
 
     square = (total, total)
 
-    tail = (dp, local - head, width)
+    tail = (dp, PARTS * local - head, width // PARTS)
 
     def pair_terms(clips, tails=0):
         return pl.pallas_call(
@@ -166,13 +181,13 @@
         )(*clips)
 
     def start_upper(noise, latents):
-        first, second = pack(noise, latents, (head, 2 * local - head))
+        first, second = pack(noise, latents, (head, 2 * PARTS * local - head))
         first, second, unused = lax.optimization_barrier((first, second, blank(square, jnp.float32)))
         first, second = lax.optimization_barrier((exchange(first, DP), second))
         return first, second, unused
 
     def start_lower(noise, latents):
-        (packed,) = pack(noise, latents, (2 * local,))
+        (packed,) = pack(noise, latents, (2 * PARTS * local,))
         clips = exchange(packed, DP)
         clips = clips[:, :head], clips[:, head:]
         return *clips, *pair_terms(clips)
@@ -194,9 +209,9 @@
         parts = exchange(spread(parts, lax.axis_size("q")), "q")
         return exchange(spread(parts, near), NEAR).reshape(total, total)
 
-    def move(cost, clips, group):
+    def move(skipped, cost, clips, group):
         moved, row, column = pl.pallas_call(
-            coupling_kernel,
+            functools.partial(coupling_kernel, skipped),
             out_shape=(jax.ShapeDtypeStruct((dp, local, width), noise.dtype), *ends),
             in_specs=[SMEM, VMEM, VMEM, VMEM],
             out_specs=(VMEM, VMEM, VMEM),
@@ -211,7 +226,7 @@
     sent = lax.ppermute(cost, "c", [(1, 0)])
     done = lax.cond(
         upper,
-        move,
+        functools.partial(move, 0),
         lambda cost, clips, group: (blank((dp, local, width), noise.dtype), *(blank(e.shape, e.dtype) for e in ends)),
         cost,
         (first, upper_noise),
@@ -220,7 +235,7 @@
     targets, row, column = lax.cond(
         upper,
         lambda done, sent, clips, group: done,
-        lambda done, sent, clips, group: move(sent, clips, group),
+        lambda done, sent, clips, group: move(local, sent, clips, group),
         done,
         sent,
         (first, second),

time: 125 us -> 123 us (0.984)
  no operation moved by 1% of the time
where the time goes in v8:
time: 123 us
  waiting for transfers between devices  67.8 us (55%)
  blocking collectives  44.4 us (36%)
  Pallas kernels  6.34 us (5%)
  starting transfers between devices  2.62 us (2%)
    ppermute x1, waiting for transfers between devices, per_device(): sent = lax.ppermute(cost, 'c', [(1, 0)])  65.4 us
    all_to_all x2, blocking collectives, exchange(): return lax.all_to_all(blocks, axes, 0, 0, tiled=True)  44.4 us
    pallas_call x1, Pallas kernels, move(): pl.pallas_call(functools.partial(coupling_kernel, skipped), out_shape=(ja...  3.05 us
  transfers between devices with their start and end apart: 2, of which 2 were waited for; matrix products, arithmetic and copies ran while one was open for 0% of the time, Pallas kernels for 0%

profile of v8, /device:TPU:8, one launch (start us, length us, event | category | flops | bytes accessed | tf_op | source)
XLA Modules:
  0.0 123.1 jit_solution(12312694487929610204)
XLA Ops:
  0.6 29.6 %conditional.5 = (bf16[16,16,256]{2,1,0:T(8,128)(2,1)S(1)}, bf16[16,112,256]{2,1,0:T(8,128)(2,1)S(1)}, f32[512,512]{1,0:T(8,128)}) conditional(s32[]{:T(128)} %convert_element_type.2, (bf16[32,16,512]{2,1,0:T(8,128)(2,1)}, bf16[32,16,512]{2,1,0:T(8,128)(2,1)}) %tuple.47, (bf16[32,16,512]{2,1,0:T(8,128)(2,1)}, bf16[32,16,512]{2,1,0:T(8,128)(2,1)}) %tuple.47), branch_computations={%region_0.0_spmd, %region_1.0_spmd} | conditional | bytes 4194328 | solution.py:201
  0.6 1.3 %branch_0_fun.9 = bf16[16,128,256]{2,1,0:T(8,128)(2,1)S(1)} custom-call(bf16[32,16,512]{2,1,0:T(8,128)(2,1)} %get-tuple-element.38.noise_ref, bf16[32,16,512]{2,1,0:T(8,128)(2,1)} %get-tuple-element.42.latents_ref), custom_call_target="tpu_custom_call" | custom-call | tf_op jit(solution)/shard_map/cond/branch_0_fun/pallas_call | solution.py:52
  2.0 26.2 %all_to_all.36 = bf16[16,128,256]{2,1,0:T(8,128)(2,1)S(1)} all-to-all(bf16[16,128,256]{2,1,0:T(8,128)(2,1)S(1)} %branch_0_fun.9), channel_id=1, replica_groups=mesh['z'=2,'q'=4,'p'=2,'h'=4,'x'=4,'c'=2] {'z','q','p'}, dimensions={0} | all-to-all | bytes 2097152 | tf_op jit(solution)/shard_map/cond/branch_0_fun/all_to_all | solution.py:113
  28.2 0.1 slice.7.rest_ref
  28.3 1.9 %branch_0_fun.10 = f32[512,512]{1,0:T(8,128)} custom-call(bf16[16,16,256]{2,1,0:T(8,128)(2,1)S(1)} %slice.6.head_ref, bf16[16,112,256]{2,1,0:T(8,128)(2,1)S(1)} %slice.7.rest_ref), custom_call_target="tpu_custom_call" | custom-call | tf_op jit(solution)/shard_map/cond/branch_0_fun/pallas_call | solution.py:174
  30.2 1.3 %collective-permute-start = (f32[512,512]{1,0:T(8,128)}, f32[512,512]{1,0:T(8,128)S(1)}, u32[]{:S(2)}, u32[]{:S(2)}) collective-permute-start(f32[512,512]{1,0:T(8,128)} %get-tuple-element.84), channel_id=1, source_target_pairs={{0,1},{2,3},{4,5},{6,7},{8,9},{10,11},{12,13},{14,15},{16,17},{18,... | collective-permute-start | bytes 3145736 | tf_op jit(solution)/shard_map/ppermute | solution.py:202
  31.6 2.4 %collective-permute-done = f32[512,512]{1,0:T(8,128)S(1)} collective-permute-done((f32[512,512]{1,0:T(8,128)}, f32[512,512]{1,0:T(8,128)S(1)}, u32[]{:S(2)}, u32[]{:S(2)}) %collective-permute-start) | collective-permute-done | bytes 1048608 | tf_op jit(solution)/shard_map/ppermute | solution.py:202
  34.0 1.3 %collective-permute-start.1 = (f32[512,512]{1,0:T(8,128)}, f32[512,512]{1,0:T(8,128)S(1)}, u32[]{:S(2)}, u32[]{:S(2)}) collective-permute-start(f32[512,512]{1,0:T(8,128)} %get-tuple-element.112), channel_id=1, source_target_pairs={{1,0},{3,2},{5,4},{7,6},{9,8},{11,10},{13,12},{15,14},{17,16},{19,... | collective-permute-start | bytes 3145736 | tf_op jit(solution)/shard_map/ppermute | solution.py:226
  35.3 65.4 %collective-permute-done.1 = f32[512,512]{1,0:T(8,128)S(1)} collective-permute-done((f32[512,512]{1,0:T(8,128)}, f32[512,512]{1,0:T(8,128)S(1)}, u32[]{:S(2)}, u32[]{:S(2)}) %collective-permute-start.1) | collective-permute-done | bytes 1048608 | tf_op jit(solution)/shard_map/ppermute | solution.py:226
  100.8 21.2 %conditional.9 = ((bf16[16,32,512]{2,1,0:T(8,128)(2,1)S(1)}, f32[1,512]{1,0:T(1,128)}, f32[1,32]{1,0:T(1,128)})) conditional(s32[]{:T(128)} %convert_element_type.2, (s32[1]{0:T(128)}, f32[512,512]{1,0:T(8,128)S(1)}, bf16[16,16,256]{2,1,0:T(8,128)(2,1)S(1)}, bf16[16,112,256]{2,1,0:T(8,128)(2,1)S(1)}) %tuple.50, (bf16[16,32,512]{2,1,0:T(8,128)(2,1)S(1)}, ...), branch_computations={%region_8.0_spmd, %region_9.0_spmd} | conditional | bytes 1048608 | solution.py:235
  100.8 3.0 %branch_0_fun.17 = (bf16[16,32,512]{2,1,0:T(8,128)(2,1)S(1)}, f32[1,512]{1,0:T(1,128)}, f32[1,32]{1,0:T(1,128)}) custom-call(s32[1]{0:T(128)} %get-tuple-element.63.group_ref, f32[512,512]{1,0:T(8,128)S(1)} %get-tuple-element.64.scores, bf16[16,16,256]{2,1,0:T(8,128)(2,1)S(1)} %get-tuple-element.65.head_ref, bf16[16,112,256]{2,1,0:T(8,128)(2,1)S(1)} %get-tuple-element.66.rest_ref), custom_call_target="tpu_custom_call" | custom-call | tf_op jit(solution)/shard_map/cond/branch_0_fun/pallas_call | solution.py:213
  103.8 18.1 %all_to_all.44 = bf16[16,32,512]{2,1,0:T(8,128)(2,1)S(1)} all-to-all(bf16[16,32,512]{2,1,0:T(8,128)(2,1)S(1)} %get-tuple-element.67), channel_id=1, replica_groups=mesh['z'=2,'q'=4,'p'=2,'h'=4,'x'=4,'c'=2] {'z','q','p'}, dimensions={0} | all-to-all | bytes 1048576 | tf_op jit(solution)/shard_map/cond/branch_0_fun/all_to_all | solution.py:113
  122.0 1.1 copy.7
  (10 shorter events, 0.1 us)
Async XLA Ops:
  30.2 3.8 %collective-permute-start = (f32[512,512]{1,0:T(8,128)}, f32[512,512]{1,0:T(8,128)S(1)}, u32[]{:S(2)}, u32[]{:S(2)}) collective-permute-start(f32[512,512]{1,0:T(8,128)} %get-tuple-element.84), channel_id=1, source_target_pairs={{0,1},{2,3},{4,5},{6,7},{8,9},{10,11},{12,13},{14,15},{16,17},{18,... | collective-permute-start | bytes 3145736 | tf_op jit(solution)/shard_map/ppermute | solution.py:202
  34.0 66.8 %collective-permute-start.1 = (f32[512,512]{1,0:T(8,128)}, f32[512,512]{1,0:T(8,128)S(1)}, u32[]{:S(2)}, u32[]{:S(2)}) collective-permute-start(f32[512,512]{1,0:T(8,128)} %get-tuple-element.112), channel_id=1, source_target_pairs={{1,0},{3,2},{5,4},{7,6},{9,8},{11,10},{13,12},{15,14},{17,16},{19,... | collective-permute-start | bytes 3145736 | tf_op jit(solution)/shard_map/ppermute | solution.py:226

commit v9 on v8

--- a/solution.py
+++ b/solution.py
@@ -9,7 +9,7 @@
 from jax.sharding import Mesh, PartitionSpec as P
 
 ITERS = 4
-PARTS = 2
+PARTS = 4
 BLUR = 0.5
 FINE = {"z": 2, "q": 4, "p": 2, "h": 4, "x": 4, "c": 2}
 DP = ("z", "q", "p")
@@ -65,9 +65,19 @@
 def noise_of(head_ref, rest_ref, local, skipped):
     sources, head, width = head_ref.shape
     tail = local - head
-    first = jnp.concatenate([head_ref[...], rest_ref[:, :tail, :]], axis=1)
-    second = rest_ref[:, tail + skipped : tail + skipped + local, :]
-    return [noise.reshape(sources * local, width) for noise in (first, second)]
+    parts = [jnp.concatenate([head_ref[...], rest_ref[:, :tail, :]], axis=1)]
+    for part in range(1, PARTS):
+        first = tail + skipped + (part - 1) * (local + skipped)
+        parts.append(rest_ref[:, first : first + local, :])
+    return [part.reshape(sources * local, width) for part in parts]
+
+
+def square_sums(parts):
+    total = 0.0
+    for part in parts:
+        wide = part.astype(jnp.float32)
+        total += wide * wide
+    return jnp.sum(total, axis=1, keepdims=True)
 
 
 def pair_kernel(factor, head_ref, rest_ref, out_ref, *tail_refs):
@@ -76,23 +86,26 @@
     total = sources * local
     tail = local - head
     noises = noise_of(head_ref, rest_ref, local, local)
-    terms = 0.0
-    for part, noise in enumerate(noises):
-        first = tail + 2 * part * local
-        latents = rest_ref[:, first : first + local, :].reshape(total, width)
-        wide = noise.astype(jnp.float32)
-        noise_norms = jnp.sum(wide * wide, axis=1, keepdims=True) * factor
-        wide = latents.astype(jnp.float32)
-        latent_norms = jnp.sum(wide * wide, axis=1, keepdims=True) * factor
-        latent_norms = jnp.transpose(jnp.broadcast_to(latent_norms, (total, 128)))[:1, :]
-        cross = lax.dot_general(
-            noise, latents, (((1,), (1,)), ((), ())), preferred_element_type=jnp.float32
-        )
-        terms += noise_norms + latent_norms - (2.0 * factor) * cross
-    out_ref[...] = terms
+    latents = [
+        rest_ref[:, first : first + local, :].reshape(total, width)
+        for first in range(tail, rest_ref.shape[1], 2 * local)
+    ]
+    noise_norms = square_sums(noises) * factor
+    latent_norms = square_sums(latents) * factor
+    latent_norms = jnp.transpose(jnp.broadcast_to(latent_norms, (total, 128)))[:1, :]
+    cross = lax.dot_general(
+        jnp.concatenate(noises, axis=1),
+        jnp.concatenate(latents, axis=1),
+        (((1,), (1,)), ((), ())),
+        preferred_element_type=jnp.float32,
+    )
+    out_ref[...] = noise_norms + latent_norms - (2.0 * factor) * cross
     for tail_ref in tail_refs:
         tail_ref[:, :tail, :] = rest_ref[:, :tail, :]
-        tail_ref[:, tail:, :] = rest_ref[:, tail + local : tail + 2 * local, :]
+        for part in range(1, PARTS):
+            first = tail + local + (part - 1) * 2 * local
+            to = tail + (part - 1) * local
+            tail_ref[:, to : to + local, :] = rest_ref[:, first : first + local, :]
 
 
 def spread_kernel(parts_ref, out_ref):
@@ -136,14 +149,12 @@
 
 def coupling_kernel(skipped, group_ref, scores, head_ref, rest_ref, moved_ref, row_ref, column_ref):
     local = column_ref.shape[1]
-    width = head_ref.shape[2]
     weights = weigh(group_ref[0], local, scores, row_ref, column_ref)
-    for part, noise in enumerate(noise_of(head_ref, rest_ref, local, skipped)):
-        moved = lax.dot_general(
-            weights, noise, (((0,), (0,)), ((), ())), preferred_element_type=jnp.float32
-        )
-        moved = moved.astype(jnp.bfloat16).reshape(-1, local, width)
-        moved_ref[:, :, part * width : (part + 1) * width] = moved
+    noise = jnp.concatenate(noise_of(head_ref, rest_ref, local, skipped), axis=1)
+    moved = lax.dot_general(
+        weights, noise, (((0,), (0,)), ((), ())), preferred_element_type=jnp.float32
+    )
+    moved_ref[...] = moved.astype(jnp.bfloat16).reshape(moved_ref.shape)
 
 
 def blank_kernel(out_ref):

time: 123 us -> 126 us (1.024)
  waiting for transfers between devices: 67.8 us -> 69.1 us
    ppermute x1, waiting for transfers between devices: 65.4 us -> 67.5 us  [per_device(): sent = lax.ppermute(cost, 'c', [(1, 0)])]
where the time goes in v9:
time: 126 us
  waiting for transfers between devices  69.1 us (55%)
  blocking collectives  43.9 us (35%)
  Pallas kernels  7.22 us (6%)
  starting transfers between devices  3.55 us (3%)
    ppermute x1, waiting for transfers between devices, per_device(): sent = lax.ppermute(cost, 'c', [(1, 0)])  67.5 us
    all_to_all x2, blocking collectives, exchange(): return lax.all_to_all(blocks, axes, 0, 0, tiled=True)  43.9 us
    pallas_call x1, Pallas kernels, move(): pl.pallas_call(functools.partial(coupling_kernel, skipped), out_shape=(ja...  4.27 us
  transfers between devices with their start and end apart: 2, of which 2 were waited for; matrix products, arithmetic and copies ran while one was open for 0% of the time, Pallas kernels for 0%

profile of v9, /device:TPU:8, one launch (start us, length us, event | category | flops | bytes accessed | tf_op | source)
XLA Modules:
  0.0 125.7 jit_solution(15956174510429298855)
XLA Ops:
  0.6 29.2 %conditional.5 = (bf16[16,16,128]{2,1,0:T(8,128)(2,1)S(1)}, bf16[16,240,128]{2,1,0:T(8,128)(2,1)S(1)}, f32[512,512]{1,0:T(8,128)}) conditional(s32[]{:T(128)} %convert_element_type.2, (bf16[32,16,512]{2,1,0:T(8,128)(2,1)}, bf16[32,16,512]{2,1,0:T(8,128)(2,1)}) %tuple.47, (bf16[32,16,512]{2,1,0:T(8,128)(2,1)}, bf16[32,16,512]{2,1,0:T(8,128)(2,1)}) %tuple.47), branch_computations={%region_0.0_spmd, %region_1.0_spmd} | conditional | bytes 4194328 | solution.py:212
  0.6 1.4 %branch_0_fun.9 = bf16[16,256,128]{2,1,0:T(8,128)(2,1)S(1)} custom-call(bf16[32,16,512]{2,1,0:T(8,128)(2,1)} %get-tuple-element.38.noise_ref, bf16[32,16,512]{2,1,0:T(8,128)(2,1)} %get-tuple-element.42.latents_ref), custom_call_target="tpu_custom_call" | custom-call | tf_op jit(solution)/shard_map/cond/branch_0_fun/pallas_call | solution.py:52
  2.1 26.2 %all_to_all.36 = bf16[16,256,128]{2,1,0:T(8,128)(2,1)S(1)} all-to-all(bf16[16,256,128]{2,1,0:T(8,128)(2,1)S(1)} %branch_0_fun.9), channel_id=1, replica_groups=mesh['z'=2,'q'=4,'p'=2,'h'=4,'x'=4,'c'=2] {'z','q','p'}, dimensions={0} | all-to-all | bytes 2097152 | tf_op jit(solution)/shard_map/cond/branch_0_fun/all_to_all | solution.py:126
  28.3 0.1 slice.7.rest_ref
  28.3 1.5 %branch_0_fun.10 = f32[512,512]{1,0:T(8,128)} custom-call(bf16[16,16,128]{2,1,0:T(8,128)(2,1)S(1)} %slice.6.head_ref, bf16[16,240,128]{2,1,0:T(8,128)(2,1)S(1)} %slice.7.rest_ref), custom_call_target="tpu_custom_call" | custom-call | tf_op jit(solution)/shard_map/cond/branch_0_fun/pallas_call | solution.py:185
  29.9 2.3 %collective-permute-start = (f32[512,512]{1,0:T(8,128)}, f32[512,512]{1,0:T(8,128)}, u32[]{:S(2)}, u32[]{:S(2)}) collective-permute-start(f32[512,512]{1,0:T(8,128)} %get-tuple-element.84), channel_id=1, source_target_pairs={{0,1},{2,3},{4,5},{6,7},{8,9},{10,11},{12,13},{14,15},{16,17},{18,... | collective-permute-start | bytes 3145736 | tf_op jit(solution)/shard_map/ppermute | solution.py:213
  32.1 1.6 %collective-permute-done = f32[512,512]{1,0:T(8,128)} collective-permute-done((f32[512,512]{1,0:T(8,128)}, f32[512,512]{1,0:T(8,128)}, u32[]{:S(2)}, u32[]{:S(2)}) %collective-permute-start) | collective-permute-done | bytes 1048608 | tf_op jit(solution)/shard_map/ppermute | solution.py:213
  33.8 1.3 %collective-permute-start.1 = (f32[512,512]{1,0:T(8,128)}, f32[512,512]{1,0:T(8,128)}, u32[]{:S(2)}, u32[]{:S(2)}) collective-permute-start(f32[512,512]{1,0:T(8,128)} %get-tuple-element.112), channel_id=1, source_target_pairs={{1,0},{3,2},{5,4},{7,6},{9,8},{11,10},{13,12},{15,14},{17,16},{19,... | collective-permute-start | bytes 3145736 | tf_op jit(solution)/shard_map/ppermute | solution.py:237
  35.1 67.5 %collective-permute-done.1 = f32[512,512]{1,0:T(8,128)} collective-permute-done((f32[512,512]{1,0:T(8,128)}, f32[512,512]{1,0:T(8,128)}, u32[]{:S(2)}, u32[]{:S(2)}) %collective-permute-start.1) | collective-permute-done | bytes 1048608 | tf_op jit(solution)/shard_map/ppermute | solution.py:237
  102.6 22.0 %conditional.9 = ((bf16[16,32,512]{2,1,0:T(8,128)(2,1)S(1)}, f32[1,512]{1,0:T(1,128)}, f32[1,32]{1,0:T(1,128)})) conditional(s32[]{:T(128)} %convert_element_type.2, (s32[1]{0:T(128)}, f32[512,512]{1,0:T(8,128)}, bf16[16,16,128]{2,1,0:T(8,128)(2,1)S(1)}, bf16[16,240,128]{2,1,0:T(8,128)(2,1)S(1)}) %tuple.50, (bf16[16,32,512]{2,1,0:T(8,128)(2,1)S(1)}, ...), branch_computations={%region_8.0_spmd, %region_9.0_spmd} | conditional | bytes 1048608 | solution.py:246
  102.6 4.3 %branch_0_fun.17 = (bf16[16,32,512]{2,1,0:T(8,128)(2,1)S(1)}, f32[1,512]{1,0:T(1,128)}, f32[1,32]{1,0:T(1,128)}) custom-call(s32[1]{0:T(128)} %get-tuple-element.63.group_ref, f32[512,512]{1,0:T(8,128)} %get-tuple-element.64.scores, bf16[16,16,128]{2,1,0:T(8,128)(2,1)S(1)} %get-tuple-element.65.head_ref, bf16[16,240,128]{2,1,0:T(8,128)(2,1)S(1)} %get-tuple-element.66.rest_ref), custom_call_target="tpu_custom_call" | custom-call | tf_op jit(solution)/shard_map/cond/branch_0_fun/pallas_call | solution.py:224
  106.9 17.7 %all_to_all.44 = bf16[16,32,512]{2,1,0:T(8,128)(2,1)S(1)} all-to-all(bf16[16,32,512]{2,1,0:T(8,128)(2,1)S(1)} %get-tuple-element.67), channel_id=1, replica_groups=mesh['z'=2,'q'=4,'p'=2,'h'=4,'x'=4,'c'=2] {'z','q','p'}, dimensions={0} | all-to-all | bytes 1048576 | tf_op jit(solution)/shard_map/cond/branch_0_fun/all_to_all | solution.py:126
  124.6 1.1 copy.7
  (10 shorter events, 0.1 us)
Async XLA Ops:
  29.9 3.9 %collective-permute-start = (f32[512,512]{1,0:T(8,128)}, f32[512,512]{1,0:T(8,128)}, u32[]{:S(2)}, u32[]{:S(2)}) collective-permute-start(f32[512,512]{1,0:T(8,128)} %get-tuple-element.84), channel_id=1, source_target_pairs={{0,1},{2,3},{4,5},{6,7},{8,9},{10,11},{12,13},{14,15},{16,17},{18,... | collective-permute-start | bytes 3145736 | tf_op jit(solution)/shard_map/ppermute | solution.py:213
  33.8 68.9 %collective-permute-start.1 = (f32[512,512]{1,0:T(8,128)}, f32[512,512]{1,0:T(8,128)}, u32[]{:S(2)}, u32[]{:S(2)}) collective-permute-start(f32[512,512]{1,0:T(8,128)} %get-tuple-element.112), channel_id=1, source_target_pairs={{1,0},{3,2},{5,4},{7,6},{9,8},{11,10},{13,12},{15,14},{17,16},{19,... | collective-permute-start | bytes 3145736 | tf_op jit(solution)/shard_map/ppermute | solution.py:237

commit v10 on v9

--- a/solution.py
+++ b/solution.py
@@ -9,7 +9,7 @@
 from jax.sharding import Mesh, PartitionSpec as P
 
 ITERS = 4
-PARTS = 4
+PARTS = 2
 BLUR = 0.5
 FINE = {"z": 2, "q": 4, "p": 2, "h": 4, "x": 4, "c": 2}
 DP = ("z", "q", "p")

time: 126 us -> 123 us (0.976)
  Pallas kernels: 7.22 us -> 5.91 us
  waiting for transfers between devices: 69.1 us -> 67.8 us
    ppermute x1, waiting for transfers between devices: 67.5 us -> 65.4 us  [per_device(): sent = lax.ppermute(cost, 'c', [(1, 0)])]
where the time goes in v10:
time: 123 us
  waiting for transfers between devices  67.8 us (55%)
  blocking collectives  44.3 us (36%)
  Pallas kernels  5.91 us (5%)
  starting transfers between devices  2.62 us (2%)
    ppermute x1, waiting for transfers between devices, per_device(): sent = lax.ppermute(cost, 'c', [(1, 0)])  65.4 us
    all_to_all x2, blocking collectives, exchange(): return lax.all_to_all(blocks, axes, 0, 0, tiled=True)  44.3 us
    pallas_call x1, Pallas kernels, move(): pl.pallas_call(functools.partial(coupling_kernel, skipped), out_shape=(ja...  3.06 us
  transfers between devices with their start and end apart: 2, of which 2 were waited for; matrix products, arithmetic and copies ran while one was open for 0% of the time, Pallas kernels for 0%

profile of v10, /device:TPU:8, one launch (start us, length us, event | category | flops | bytes accessed | tf_op | source)
XLA Modules:
  0.0 122.6 jit_solution(17932902542163202196)
XLA Ops:
  0.6 29.2 %conditional.5 = (bf16[16,16,256]{2,1,0:T(8,128)(2,1)S(1)}, bf16[16,112,256]{2,1,0:T(8,128)(2,1)S(1)}, f32[512,512]{1,0:T(8,128)}) conditional(s32[]{:T(128)} %convert_element_type.2, (bf16[32,16,512]{2,1,0:T(8,128)(2,1)}, bf16[32,16,512]{2,1,0:T(8,128)(2,1)}) %tuple.47, (bf16[32,16,512]{2,1,0:T(8,128)(2,1)}, bf16[32,16,512]{2,1,0:T(8,128)(2,1)}) %tuple.47), branch_computations={%region_0.0_spmd, %region_1.0_spmd} | conditional | bytes 4194328 | solution.py:212
  0.6 1.3 %branch_0_fun.9 = bf16[16,128,256]{2,1,0:T(8,128)(2,1)S(1)} custom-call(bf16[32,16,512]{2,1,0:T(8,128)(2,1)} %get-tuple-element.38.noise_ref, bf16[32,16,512]{2,1,0:T(8,128)(2,1)} %get-tuple-element.42.latents_ref), custom_call_target="tpu_custom_call" | custom-call | tf_op jit(solution)/shard_map/cond/branch_0_fun/pallas_call | solution.py:52
  2.0 26.2 %all_to_all.36 = bf16[16,128,256]{2,1,0:T(8,128)(2,1)S(1)} all-to-all(bf16[16,128,256]{2,1,0:T(8,128)(2,1)S(1)} %branch_0_fun.9), channel_id=1, replica_groups=mesh['z'=2,'q'=4,'p'=2,'h'=4,'x'=4,'c'=2] {'z','q','p'}, dimensions={0} | all-to-all | bytes 2097152 | tf_op jit(solution)/shard_map/cond/branch_0_fun/all_to_all | solution.py:126
  28.2 0.1 slice.7.rest_ref
  28.3 1.5 %branch_0_fun.10 = f32[512,512]{1,0:T(8,128)} custom-call(bf16[16,16,256]{2,1,0:T(8,128)(2,1)S(1)} %slice.6.head_ref, bf16[16,112,256]{2,1,0:T(8,128)(2,1)S(1)} %slice.7.rest_ref), custom_call_target="tpu_custom_call" | custom-call | tf_op jit(solution)/shard_map/cond/branch_0_fun/pallas_call | solution.py:185
  29.8 1.3 %collective-permute-start = (f32[512,512]{1,0:T(8,128)}, f32[512,512]{1,0:T(8,128)S(1)}, u32[]{:S(2)}, u32[]{:S(2)}) collective-permute-start(f32[512,512]{1,0:T(8,128)} %get-tuple-element.84), channel_id=1, source_target_pairs={{0,1},{2,3},{4,5},{6,7},{8,9},{10,11},{12,13},{14,15},{16,17},{18,... | collective-permute-start | bytes 3145736 | tf_op jit(solution)/shard_map/ppermute | solution.py:213
  31.2 2.4 %collective-permute-done = f32[512,512]{1,0:T(8,128)S(1)} collective-permute-done((f32[512,512]{1,0:T(8,128)}, f32[512,512]{1,0:T(8,128)S(1)}, u32[]{:S(2)}, u32[]{:S(2)}) %collective-permute-start) | collective-permute-done | bytes 1048608 | tf_op jit(solution)/shard_map/ppermute | solution.py:213
  33.6 1.3 %collective-permute-start.1 = (f32[512,512]{1,0:T(8,128)}, f32[512,512]{1,0:T(8,128)S(1)}, u32[]{:S(2)}, u32[]{:S(2)}) collective-permute-start(f32[512,512]{1,0:T(8,128)} %get-tuple-element.112), channel_id=1, source_target_pairs={{1,0},{3,2},{5,4},{7,6},{9,8},{11,10},{13,12},{15,14},{17,16},{19,... | collective-permute-start | bytes 3145736 | tf_op jit(solution)/shard_map/ppermute | solution.py:237
  34.9 65.4 %collective-permute-done.1 = f32[512,512]{1,0:T(8,128)S(1)} collective-permute-done((f32[512,512]{1,0:T(8,128)}, f32[512,512]{1,0:T(8,128)S(1)}, u32[]{:S(2)}, u32[]{:S(2)}) %collective-permute-start.1) | collective-permute-done | bytes 1048608 | tf_op jit(solution)/shard_map/ppermute | solution.py:237
  100.3 21.2 %conditional.9 = ((bf16[16,32,512]{2,1,0:T(8,128)(2,1)S(1)}, f32[1,512]{1,0:T(1,128)}, f32[1,32]{1,0:T(1,128)})) conditional(s32[]{:T(128)} %convert_element_type.2, (s32[1]{0:T(128)}, f32[512,512]{1,0:T(8,128)S(1)}, bf16[16,16,256]{2,1,0:T(8,128)(2,1)S(1)}, bf16[16,112,256]{2,1,0:T(8,128)(2,1)S(1)}) %tuple.50, (bf16[16,32,512]{2,1,0:T(8,128)(2,1)S(1)}, ...), branch_computations={%region_8.0_spmd, %region_9.0_spmd} | conditional | bytes 1048608 | solution.py:246
  100.3 3.1 %branch_0_fun.17 = (bf16[16,32,512]{2,1,0:T(8,128)(2,1)S(1)}, f32[1,512]{1,0:T(1,128)}, f32[1,32]{1,0:T(1,128)}) custom-call(s32[1]{0:T(128)} %get-tuple-element.63.group_ref, f32[512,512]{1,0:T(8,128)S(1)} %get-tuple-element.64.scores, bf16[16,16,256]{2,1,0:T(8,128)(2,1)S(1)} %get-tuple-element.65.head_ref, bf16[16,112,256]{2,1,0:T(8,128)(2,1)S(1)} %get-tuple-element.66.rest_ref), custom_call_target="tpu_custom_call" | custom-call | tf_op jit(solution)/shard_map/cond/branch_0_fun/pallas_call | solution.py:224
  103.4 18.1 %all_to_all.44 = bf16[16,32,512]{2,1,0:T(8,128)(2,1)S(1)} all-to-all(bf16[16,32,512]{2,1,0:T(8,128)(2,1)S(1)} %get-tuple-element.67), channel_id=1, replica_groups=mesh['z'=2,'q'=4,'p'=2,'h'=4,'x'=4,'c'=2] {'z','q','p'}, dimensions={0} | all-to-all | bytes 1048576 | tf_op jit(solution)/shard_map/cond/branch_0_fun/all_to_all | solution.py:126
  121.5 1.1 copy.7
  (10 shorter events, 0.1 us)
Async XLA Ops:
  29.8 3.8 %collective-permute-start = (f32[512,512]{1,0:T(8,128)}, f32[512,512]{1,0:T(8,128)S(1)}, u32[]{:S(2)}, u32[]{:S(2)}) collective-permute-start(f32[512,512]{1,0:T(8,128)} %get-tuple-element.84), channel_id=1, source_target_pairs={{0,1},{2,3},{4,5},{6,7},{8,9},{10,11},{12,13},{14,15},{16,17},{18,... | collective-permute-start | bytes 3145736 | tf_op jit(solution)/shard_map/ppermute | solution.py:213
  33.6 66.8 %collective-permute-start.1 = (f32[512,512]{1,0:T(8,128)}, f32[512,512]{1,0:T(8,128)S(1)}, u32[]{:S(2)}, u32[]{:S(2)}) collective-permute-start(f32[512,512]{1,0:T(8,128)} %get-tuple-element.112), channel_id=1, source_target_pairs={{1,0},{3,2},{5,4},{7,6},{9,8},{11,10},{13,12},{15,14},{17,16},{19,... | collective-permute-start | bytes 3145736 | tf_op jit(solution)/shard_map/ppermute | solution.py:237

commit v11 on v10

--- a/solution.py
+++ b/solution.py
@@ -216,8 +216,8 @@
     def reduce_cost(terms, received):
         summed = terms + received
         parts = exchange(summed.reshape(near, total // near, total), NEAR)
+        parts = exchange(spread(parts, lax.axis_size("q")), "q")
         parts = exchange(spread(parts, lax.axis_size("h")), "h")
-        parts = exchange(spread(parts, lax.axis_size("q")), "q")
         return exchange(spread(parts, near), NEAR).reshape(total, total)
 
     def move(skipped, cost, clips, group):

time: 123 us -> 123 us (level)
  no operation moved by 1% of the time
where the time goes in v11:
time: 123 us
  waiting for transfers between devices  67.8 us (55%)
  blocking collectives  44.2 us (36%)
  Pallas kernels  5.91 us (5%)
  starting transfers between devices  2.62 us (2%)
    ppermute x1, waiting for transfers between devices, per_device(): sent = lax.ppermute(cost, 'c', [(1, 0)])  65.4 us
    all_to_all x2, blocking collectives, exchange(): return lax.all_to_all(blocks, axes, 0, 0, tiled=True)  44.2 us
    pallas_call x1, Pallas kernels, move(): pl.pallas_call(functools.partial(coupling_kernel, skipped), out_shape=(ja...  3.06 us
  transfers between devices with their start and end apart: 2, of which 2 were waited for; matrix products, arithmetic and copies ran while one was open for 0% of the time, Pallas kernels for 0%

profile of v11, /device:TPU:8, one launch (start us, length us, event | category | flops | bytes accessed | tf_op | source)
XLA Modules:
  0.0 122.5 jit_solution(6621918854318137849)
XLA Ops:
  0.6 29.2 %conditional.5 = (bf16[16,16,256]{2,1,0:T(8,128)(2,1)S(1)}, bf16[16,112,256]{2,1,0:T(8,128)(2,1)S(1)}, f32[512,512]{1,0:T(8,128)}) conditional(s32[]{:T(128)} %convert_element_type.2, (bf16[32,16,512]{2,1,0:T(8,128)(2,1)}, bf16[32,16,512]{2,1,0:T(8,128)(2,1)}) %tuple.47, (bf16[32,16,512]{2,1,0:T(8,128)(2,1)}, bf16[32,16,512]{2,1,0:T(8,128)(2,1)}) %tuple.47), branch_computations={%region_0.0_spmd, %region_1.0_spmd} | conditional | bytes 4194328 | solution.py:212
  0.6 1.3 %branch_0_fun.9 = bf16[16,128,256]{2,1,0:T(8,128)(2,1)S(1)} custom-call(bf16[32,16,512]{2,1,0:T(8,128)(2,1)} %get-tuple-element.38.noise_ref, bf16[32,16,512]{2,1,0:T(8,128)(2,1)} %get-tuple-element.42.latents_ref), custom_call_target="tpu_custom_call" | custom-call | tf_op jit(solution)/shard_map/cond/branch_0_fun/pallas_call | solution.py:52
  2.0 26.2 %all_to_all.36 = bf16[16,128,256]{2,1,0:T(8,128)(2,1)S(1)} all-to-all(bf16[16,128,256]{2,1,0:T(8,128)(2,1)S(1)} %branch_0_fun.9), channel_id=1, replica_groups=mesh['z'=2,'q'=4,'p'=2,'h'=4,'x'=4,'c'=2] {'z','q','p'}, dimensions={0} | all-to-all | bytes 2097152 | tf_op jit(solution)/shard_map/cond/branch_0_fun/all_to_all | solution.py:126
  28.2 0.1 slice.7.rest_ref
  28.3 1.5 %branch_0_fun.10 = f32[512,512]{1,0:T(8,128)} custom-call(bf16[16,16,256]{2,1,0:T(8,128)(2,1)S(1)} %slice.6.head_ref, bf16[16,112,256]{2,1,0:T(8,128)(2,1)S(1)} %slice.7.rest_ref), custom_call_target="tpu_custom_call" | custom-call | tf_op jit(solution)/shard_map/cond/branch_0_fun/pallas_call | solution.py:185
  29.8 1.3 %collective-permute-start = (f32[512,512]{1,0:T(8,128)}, f32[512,512]{1,0:T(8,128)S(1)}, u32[]{:S(2)}, u32[]{:S(2)}) collective-permute-start(f32[512,512]{1,0:T(8,128)} %get-tuple-element.84), channel_id=1, source_target_pairs={{0,1},{2,3},{4,5},{6,7},{8,9},{10,11},{12,13},{14,15},{16,17},{18,... | collective-permute-start | bytes 3145736 | tf_op jit(solution)/shard_map/ppermute | solution.py:213
  31.2 2.4 %collective-permute-done = f32[512,512]{1,0:T(8,128)S(1)} collective-permute-done((f32[512,512]{1,0:T(8,128)}, f32[512,512]{1,0:T(8,128)S(1)}, u32[]{:S(2)}, u32[]{:S(2)}) %collective-permute-start) | collective-permute-done | bytes 1048608 | tf_op jit(solution)/shard_map/ppermute | solution.py:213
  33.6 1.3 %collective-permute-start.1 = (f32[512,512]{1,0:T(8,128)}, f32[512,512]{1,0:T(8,128)S(1)}, u32[]{:S(2)}, u32[]{:S(2)}) collective-permute-start(f32[512,512]{1,0:T(8,128)} %get-tuple-element.112), channel_id=1, source_target_pairs={{1,0},{3,2},{5,4},{7,6},{9,8},{11,10},{13,12},{15,14},{17,16},{19,... | collective-permute-start | bytes 3145736 | tf_op jit(solution)/shard_map/ppermute | solution.py:237
  34.9 65.4 %collective-permute-done.1 = f32[512,512]{1,0:T(8,128)S(1)} collective-permute-done((f32[512,512]{1,0:T(8,128)}, f32[512,512]{1,0:T(8,128)S(1)}, u32[]{:S(2)}, u32[]{:S(2)}) %collective-permute-start.1) | collective-permute-done | bytes 1048608 | tf_op jit(solution)/shard_map/ppermute | solution.py:237
  100.3 21.1 %conditional.9 = ((bf16[16,32,512]{2,1,0:T(8,128)(2,1)S(1)}, f32[1,512]{1,0:T(1,128)}, f32[1,32]{1,0:T(1,128)})) conditional(s32[]{:T(128)} %convert_element_type.2, (s32[1]{0:T(128)}, f32[512,512]{1,0:T(8,128)S(1)}, bf16[16,16,256]{2,1,0:T(8,128)(2,1)S(1)}, bf16[16,112,256]{2,1,0:T(8,128)(2,1)S(1)}) %tuple.50, (bf16[16,32,512]{2,1,0:T(8,128)(2,1)S(1)}, ...), branch_computations={%region_8.0_spmd, %region_9.0_spmd} | conditional | bytes 1048608 | solution.py:246
  100.3 3.1 %branch_0_fun.17 = (bf16[16,32,512]{2,1,0:T(8,128)(2,1)S(1)}, f32[1,512]{1,0:T(1,128)}, f32[1,32]{1,0:T(1,128)}) custom-call(s32[1]{0:T(128)} %get-tuple-element.63.group_ref, f32[512,512]{1,0:T(8,128)S(1)} %get-tuple-element.64.scores, bf16[16,16,256]{2,1,0:T(8,128)(2,1)S(1)} %get-tuple-element.65.head_ref, bf16[16,112,256]{2,1,0:T(8,128)(2,1)S(1)} %get-tuple-element.66.rest_ref), custom_call_target="tpu_custom_call" | custom-call | tf_op jit(solution)/shard_map/cond/branch_0_fun/pallas_call | solution.py:224
  103.4 18.0 %all_to_all.44 = bf16[16,32,512]{2,1,0:T(8,128)(2,1)S(1)} all-to-all(bf16[16,32,512]{2,1,0:T(8,128)(2,1)S(1)} %get-tuple-element.67), channel_id=1, replica_groups=mesh['z'=2,'q'=4,'p'=2,'h'=4,'x'=4,'c'=2] {'z','q','p'}, dimensions={0} | all-to-all | bytes 1048576 | tf_op jit(solution)/shard_map/cond/branch_0_fun/all_to_all | solution.py:126
  121.4 1.1 copy.7
  (10 shorter events, 0.1 us)
Async XLA Ops:
  29.8 3.8 %collective-permute-start = (f32[512,512]{1,0:T(8,128)}, f32[512,512]{1,0:T(8,128)S(1)}, u32[]{:S(2)}, u32[]{:S(2)}) collective-permute-start(f32[512,512]{1,0:T(8,128)} %get-tuple-element.84), channel_id=1, source_target_pairs={{0,1},{2,3},{4,5},{6,7},{8,9},{10,11},{12,13},{14,15},{16,17},{18,... | collective-permute-start | bytes 3145736 | tf_op jit(solution)/shard_map/ppermute | solution.py:213
  33.6 66.8 %collective-permute-start.1 = (f32[512,512]{1,0:T(8,128)}, f32[512,512]{1,0:T(8,128)S(1)}, u32[]{:S(2)}, u32[]{:S(2)}) collective-permute-start(f32[512,512]{1,0:T(8,128)} %get-tuple-element.112), channel_id=1, source_target_pairs={{1,0},{3,2},{5,4},{7,6},{9,8},{11,10},{13,12},{15,14},{17,16},{19,... | collective-permute-start | bytes 3145736 | tf_op jit(solution)/shard_map/ppermute | solution.py:237

commit v12 on v10

--- a/solution.py
+++ b/solution.py
@@ -62,6 +62,31 @@
     )(*(pltpu.with_memory_space_constraint(given, pltpu.HBM) for given in (noise, latents)))
 
 
+def unpack_kernel(moved_ref, out_ref, held, written):
+    half = moved_ref.shape[1] // 2
+    copies = []
+    for k in range(2):
+        clips = pl.ds(k * half, half)
+        held[clips] = jnp.swapaxes(moved_ref[:, clips, :], 0, 1)
+        copies.append(pltpu.make_async_copy(held.at[clips], out_ref.at[clips], written.at[k]))
+        copies[k].start()
+    for copy in copies:
+        copy.wait()
+
+
+def unpack(moved):
+    channels, local, width = moved.shape
+    shape = (local, channels, width)
+    return pl.pallas_call(
+        unpack_kernel,
+        out_shape=jax.ShapeDtypeStruct(shape, moved.dtype),
+        in_specs=[VMEM],
+        out_specs=ANY,
+        scratch_shapes=[pltpu.VMEM(shape, moved.dtype), pltpu.SemaphoreType.DMA((2,))],
+        compiler_params=LIMIT,
+    )(moved)
+
+
 def noise_of(head_ref, rest_ref, local, skipped):
     sources, head, width = head_ref.shape
     tail = local - head
@@ -252,7 +277,7 @@
         (first, second),
         group,
     )
-    return (targets.swapaxes(0, 1), row.reshape(total), column.reshape(local))
+    return (unpack(targets), row.reshape(total), column.reshape(local))
 
 
 def solution(mesh):

time: 123 us -> 123 us (level)
  no operation moved by 1% of the time
where the time goes in v12:
time: 123 us; the launch traced here: 122 us
  waiting for transfers between devices  67.8 us (55%)
  blocking collectives  44.3 us (36%)
  Pallas kernels  6.78 us (6%)
  starting transfers between devices  2.62 us (2%)
    ppermute x1, waiting for transfers between devices, per_device(): sent = lax.ppermute(cost, 'c', [(1, 0)])  65.4 us
    all_to_all x2, blocking collectives, exchange(): return lax.all_to_all(blocks, axes, 0, 0, tiled=True)  44.3 us
    pallas_call x1, Pallas kernels, move(): pl.pallas_call(functools.partial(coupling_kernel, skipped), out_shape=(ja...  3.06 us
  transfers between devices with their start and end apart: 2, of which 2 were waited for; matrix products, arithmetic and copies ran while one was open for 0% of the time, Pallas kernels for 0%

profile of v12, /device:TPU:8, one launch (start us, length us, event | category | flops | bytes accessed | tf_op | source)
XLA Modules:
  0.0 122.4 jit_solution(11900393803290669742)
XLA Ops:
  0.6 29.2 %conditional.5 = (bf16[16,16,256]{2,1,0:T(8,128)(2,1)S(1)}, bf16[16,112,256]{2,1,0:T(8,128)(2,1)S(1)}, f32[512,512]{1,0:T(8,128)}) conditional(s32[]{:T(128)} %convert_element_type.2, (bf16[32,16,512]{2,1,0:T(8,128)(2,1)}, bf16[32,16,512]{2,1,0:T(8,128)(2,1)}) %tuple.47, (bf16[32,16,512]{2,1,0:T(8,128)(2,1)}, bf16[32,16,512]{2,1,0:T(8,128)(2,1)}) %tuple.47), branch_computations={%region_0.0_spmd, %region_1.0_spmd} | conditional | bytes 4194328 | solution.py:237
  0.6 1.3 %branch_0_fun.9 = bf16[16,128,256]{2,1,0:T(8,128)(2,1)S(1)} custom-call(bf16[32,16,512]{2,1,0:T(8,128)(2,1)} %get-tuple-element.38.noise_ref, bf16[32,16,512]{2,1,0:T(8,128)(2,1)} %get-tuple-element.42.latents_ref), custom_call_target="tpu_custom_call" | custom-call | tf_op jit(solution)/shard_map/cond/branch_0_fun/pallas_call | solution.py:52
  2.0 26.2 %all_to_all.36 = bf16[16,128,256]{2,1,0:T(8,128)(2,1)S(1)} all-to-all(bf16[16,128,256]{2,1,0:T(8,128)(2,1)S(1)} %branch_0_fun.9), channel_id=1, replica_groups=mesh['z'=2,'q'=4,'p'=2,'h'=4,'x'=4,'c'=2] {'z','q','p'}, dimensions={0} | all-to-all | bytes 2097152 | tf_op jit(solution)/shard_map/cond/branch_0_fun/all_to_all | solution.py:151
  28.2 0.1 slice.7.rest_ref
  28.3 1.5 %branch_0_fun.10 = f32[512,512]{1,0:T(8,128)} custom-call(bf16[16,16,256]{2,1,0:T(8,128)(2,1)S(1)} %slice.6.head_ref, bf16[16,112,256]{2,1,0:T(8,128)(2,1)S(1)} %slice.7.rest_ref), custom_call_target="tpu_custom_call" | custom-call | tf_op jit(solution)/shard_map/cond/branch_0_fun/pallas_call | solution.py:210
  29.8 1.3 %collective-permute-start = (f32[512,512]{1,0:T(8,128)}, f32[512,512]{1,0:T(8,128)S(1)}, u32[]{:S(2)}, u32[]{:S(2)}) collective-permute-start(f32[512,512]{1,0:T(8,128)} %get-tuple-element.84), channel_id=1, source_target_pairs={{0,1},{2,3},{4,5},{6,7},{8,9},{10,11},{12,13},{14,15},{16,17},{18,... | collective-permute-start | bytes 3145736 | tf_op jit(solution)/shard_map/ppermute | solution.py:238
  31.2 2.4 %collective-permute-done = f32[512,512]{1,0:T(8,128)S(1)} collective-permute-done((f32[512,512]{1,0:T(8,128)}, f32[512,512]{1,0:T(8,128)S(1)}, u32[]{:S(2)}, u32[]{:S(2)}) %collective-permute-start) | collective-permute-done | bytes 1048608 | tf_op jit(solution)/shard_map/ppermute | solution.py:238
  33.6 1.3 %collective-permute-start.1 = (f32[512,512]{1,0:T(8,128)}, f32[512,512]{1,0:T(8,128)S(1)}, u32[]{:S(2)}, u32[]{:S(2)}) collective-permute-start(f32[512,512]{1,0:T(8,128)} %get-tuple-element.112), channel_id=1, source_target_pairs={{1,0},{3,2},{5,4},{7,6},{9,8},{11,10},{13,12},{15,14},{17,16},{19,... | collective-permute-start | bytes 3145736 | tf_op jit(solution)/shard_map/ppermute | solution.py:262
  34.9 65.4 %collective-permute-done.1 = f32[512,512]{1,0:T(8,128)S(1)} collective-permute-done((f32[512,512]{1,0:T(8,128)}, f32[512,512]{1,0:T(8,128)S(1)}, u32[]{:S(2)}, u32[]{:S(2)}) %collective-permute-start.1) | collective-permute-done | bytes 1048608 | tf_op jit(solution)/shard_map/ppermute | solution.py:262
  100.3 21.2 %conditional.9 = ((bf16[16,32,512]{2,1,0:T(8,128)(2,1)S(1)}, f32[1,512]{1,0:T(1,128)}, f32[1,32]{1,0:T(1,128)})) conditional(s32[]{:T(128)} %convert_element_type.2, (s32[1]{0:T(128)}, f32[512,512]{1,0:T(8,128)S(1)}, bf16[16,16,256]{2,1,0:T(8,128)(2,1)S(1)}, bf16[16,112,256]{2,1,0:T(8,128)(2,1)S(1)}) %tuple.50, (bf16[16,32,512]{2,1,0:T(8,128)(2,1)S(1)}, ...), branch_computations={%region_8.0_spmd, %region_9.0_spmd} | conditional | bytes 1048608 | solution.py:271
  100.3 3.1 %branch_0_fun.17 = (bf16[16,32,512]{2,1,0:T(8,128)(2,1)S(1)}, f32[1,512]{1,0:T(1,128)}, f32[1,32]{1,0:T(1,128)}) custom-call(s32[1]{0:T(128)} %get-tuple-element.63.group_ref, f32[512,512]{1,0:T(8,128)S(1)} %get-tuple-element.64.scores, bf16[16,16,256]{2,1,0:T(8,128)(2,1)S(1)} %get-tuple-element.65.head_ref, bf16[16,112,256]{2,1,0:T(8,128)(2,1)S(1)} %get-tuple-element.66.rest_ref), custom_call_target="tpu_custom_call" | custom-call | tf_op jit(solution)/shard_map/cond/branch_0_fun/pallas_call | solution.py:249
  103.4 18.1 %all_to_all.44 = bf16[16,32,512]{2,1,0:T(8,128)(2,1)S(1)} all-to-all(bf16[16,32,512]{2,1,0:T(8,128)(2,1)S(1)} %get-tuple-element.67), channel_id=1, replica_groups=mesh['z'=2,'q'=4,'p'=2,'h'=4,'x'=4,'c'=2] {'z','q','p'}, dimensions={0} | all-to-all | bytes 1048576 | tf_op jit(solution)/shard_map/cond/branch_0_fun/all_to_all | solution.py:151
  121.5 0.9 shard_map.49
  (10 shorter events, 0.1 us)
Async XLA Ops:
  29.8 3.8 %collective-permute-start = (f32[512,512]{1,0:T(8,128)}, f32[512,512]{1,0:T(8,128)S(1)}, u32[]{:S(2)}, u32[]{:S(2)}) collective-permute-start(f32[512,512]{1,0:T(8,128)} %get-tuple-element.84), channel_id=1, source_target_pairs={{0,1},{2,3},{4,5},{6,7},{8,9},{10,11},{12,13},{14,15},{16,17},{18,... | collective-permute-start | bytes 3145736 | tf_op jit(solution)/shard_map/ppermute | solution.py:238
  33.6 66.8 %collective-permute-start.1 = (f32[512,512]{1,0:T(8,128)}, f32[512,512]{1,0:T(8,128)S(1)}, u32[]{:S(2)}, u32[]{:S(2)}) collective-permute-start(f32[512,512]{1,0:T(8,128)} %get-tuple-element.112), channel_id=1, source_target_pairs={{1,0},{3,2},{5,4},{7,6},{9,8},{11,10},{13,12},{15,14},{17,16},{19,... | collective-permute-start | bytes 3145736 | tf_op jit(solution)/shard_map/ppermute | solution.py:262

commit v13 on v10

--- a/solution.py
+++ b/solution.py
@@ -19,7 +19,7 @@
 HBM = pl.BlockSpec(memory_space=pltpu.HBM)
 VMEM = pl.BlockSpec(memory_space=pltpu.VMEM)
 SMEM = pl.BlockSpec(memory_space=pltpu.SMEM)
-LIMIT = pltpu.CompilerParams(vmem_limit_bytes=32 * 1024 * 1024)
+LIMIT = pltpu.CompilerParams(vmem_limit_bytes=12 * 1024 * 1024)
 
 
 def pack_kernel(noise_ref, latents_ref, *rest):

time: 123 us -> 123 us (level)
  no operation moved by 1% of the time
where the time goes in v13:
time: 123 us
  waiting for transfers between devices  67.8 us (55%)
  blocking collectives  44.3 us (36%)
  Pallas kernels  5.91 us (5%)
  starting transfers between devices  2.62 us (2%)
    ppermute x1, waiting for transfers between devices, per_device(): sent = lax.ppermute(cost, 'c', [(1, 0)])  65.4 us
    all_to_all x2, blocking collectives, exchange(): return lax.all_to_all(blocks, axes, 0, 0, tiled=True)  44.3 us
    pallas_call x1, Pallas kernels, move(): pl.pallas_call(functools.partial(coupling_kernel, skipped), out_shape=(ja...  3.06 us
  transfers between devices with their start and end apart: 2, of which 2 were waited for; matrix products, arithmetic and copies ran while one was open for 0% of the time, Pallas kernels for 0%

profile of v13, /device:TPU:8, one launch (start us, length us, event | category | flops | bytes accessed | tf_op | source)
XLA Modules:
  0.0 122.6 jit_solution(10774262665293054037)
XLA Ops:
  0.6 29.2 %conditional.5 = (bf16[16,16,256]{2,1,0:T(8,128)(2,1)S(1)}, bf16[16,112,256]{2,1,0:T(8,128)(2,1)S(1)}, f32[512,512]{1,0:T(8,128)}) conditional(s32[]{:T(128)} %convert_element_type.2, (bf16[32,16,512]{2,1,0:T(8,128)(2,1)}, bf16[32,16,512]{2,1,0:T(8,128)(2,1)}) %tuple.47, (bf16[32,16,512]{2,1,0:T(8,128)(2,1)}, bf16[32,16,512]{2,1,0:T(8,128)(2,1)}) %tuple.47), branch_computations={%region_0.0_spmd, %region_1.0_spmd} | conditional | bytes 4194328 | solution.py:212
  0.6 1.3 %branch_0_fun.9 = bf16[16,128,256]{2,1,0:T(8,128)(2,1)S(1)} custom-call(bf16[32,16,512]{2,1,0:T(8,128)(2,1)} %get-tuple-element.38.noise_ref, bf16[32,16,512]{2,1,0:T(8,128)(2,1)} %get-tuple-element.42.latents_ref), custom_call_target="tpu_custom_call" | custom-call | tf_op jit(solution)/shard_map/cond/branch_0_fun/pallas_call | solution.py:52
  2.0 26.2 %all_to_all.36 = bf16[16,128,256]{2,1,0:T(8,128)(2,1)S(1)} all-to-all(bf16[16,128,256]{2,1,0:T(8,128)(2,1)S(1)} %branch_0_fun.9), channel_id=1, replica_groups=mesh['z'=2,'q'=4,'p'=2,'h'=4,'x'=4,'c'=2] {'z','q','p'}, dimensions={0} | all-to-all | bytes 2097152 | tf_op jit(solution)/shard_map/cond/branch_0_fun/all_to_all | solution.py:126
  28.2 0.1 slice.7.rest_ref
  28.3 1.5 %branch_0_fun.10 = f32[512,512]{1,0:T(8,128)} custom-call(bf16[16,16,256]{2,1,0:T(8,128)(2,1)S(1)} %slice.6.head_ref, bf16[16,112,256]{2,1,0:T(8,128)(2,1)S(1)} %slice.7.rest_ref), custom_call_target="tpu_custom_call" | custom-call | tf_op jit(solution)/shard_map/cond/branch_0_fun/pallas_call | solution.py:185
  29.8 1.3 %collective-permute-start = (f32[512,512]{1,0:T(8,128)}, f32[512,512]{1,0:T(8,128)S(1)}, u32[]{:S(2)}, u32[]{:S(2)}) collective-permute-start(f32[512,512]{1,0:T(8,128)} %get-tuple-element.84), channel_id=1, source_target_pairs={{0,1},{2,3},{4,5},{6,7},{8,9},{10,11},{12,13},{14,15},{16,17},{18,... | collective-permute-start | bytes 3145736 | tf_op jit(solution)/shard_map/ppermute | solution.py:213
  31.2 2.4 %collective-permute-done = f32[512,512]{1,0:T(8,128)S(1)} collective-permute-done((f32[512,512]{1,0:T(8,128)}, f32[512,512]{1,0:T(8,128)S(1)}, u32[]{:S(2)}, u32[]{:S(2)}) %collective-permute-start) | collective-permute-done | bytes 1048608 | tf_op jit(solution)/shard_map/ppermute | solution.py:213
  33.6 1.3 %collective-permute-start.1 = (f32[512,512]{1,0:T(8,128)}, f32[512,512]{1,0:T(8,128)S(1)}, u32[]{:S(2)}, u32[]{:S(2)}) collective-permute-start(f32[512,512]{1,0:T(8,128)} %get-tuple-element.112), channel_id=1, source_target_pairs={{1,0},{3,2},{5,4},{7,6},{9,8},{11,10},{13,12},{15,14},{17,16},{19,... | collective-permute-start | bytes 3145736 | tf_op jit(solution)/shard_map/ppermute | solution.py:237
  34.9 65.4 %collective-permute-done.1 = f32[512,512]{1,0:T(8,128)S(1)} collective-permute-done((f32[512,512]{1,0:T(8,128)}, f32[512,512]{1,0:T(8,128)S(1)}, u32[]{:S(2)}, u32[]{:S(2)}) %collective-permute-start.1) | collective-permute-done | bytes 1048608 | tf_op jit(solution)/shard_map/ppermute | solution.py:237
  100.3 21.2 %conditional.9 = ((bf16[16,32,512]{2,1,0:T(8,128)(2,1)S(1)}, f32[1,512]{1,0:T(1,128)}, f32[1,32]{1,0:T(1,128)})) conditional(s32[]{:T(128)} %convert_element_type.2, (s32[1]{0:T(128)}, f32[512,512]{1,0:T(8,128)S(1)}, bf16[16,16,256]{2,1,0:T(8,128)(2,1)S(1)}, bf16[16,112,256]{2,1,0:T(8,128)(2,1)S(1)}) %tuple.50, (bf16[16,32,512]{2,1,0:T(8,128)(2,1)S(1)}, ...), branch_computations={%region_8.0_spmd, %region_9.0_spmd} | conditional | bytes 1048608 | solution.py:246
  100.3 3.1 %branch_0_fun.17 = (bf16[16,32,512]{2,1,0:T(8,128)(2,1)S(1)}, f32[1,512]{1,0:T(1,128)}, f32[1,32]{1,0:T(1,128)}) custom-call(s32[1]{0:T(128)} %get-tuple-element.63.group_ref, f32[512,512]{1,0:T(8,128)S(1)} %get-tuple-element.64.scores, bf16[16,16,256]{2,1,0:T(8,128)(2,1)S(1)} %get-tuple-element.65.head_ref, bf16[16,112,256]{2,1,0:T(8,128)(2,1)S(1)} %get-tuple-element.66.rest_ref), custom_call_target="tpu_custom_call" | custom-call | tf_op jit(solution)/shard_map/cond/branch_0_fun/pallas_call | solution.py:224
  103.4 18.1 %all_to_all.44 = bf16[16,32,512]{2,1,0:T(8,128)(2,1)S(1)} all-to-all(bf16[16,32,512]{2,1,0:T(8,128)(2,1)S(1)} %get-tuple-element.67), channel_id=1, replica_groups=mesh['z'=2,'q'=4,'p'=2,'h'=4,'x'=4,'c'=2] {'z','q','p'}, dimensions={0} | all-to-all | bytes 1048576 | tf_op jit(solution)/shard_map/cond/branch_0_fun/all_to_all | solution.py:126
  121.5 1.1 copy.7
  (10 shorter events, 0.1 us)
Async XLA Ops:
  29.8 3.8 %collective-permute-start = (f32[512,512]{1,0:T(8,128)}, f32[512,512]{1,0:T(8,128)S(1)}, u32[]{:S(2)}, u32[]{:S(2)}) collective-permute-start(f32[512,512]{1,0:T(8,128)} %get-tuple-element.84), channel_id=1, source_target_pairs={{0,1},{2,3},{4,5},{6,7},{8,9},{10,11},{12,13},{14,15},{16,17},{18,... | collective-permute-start | bytes 3145736 | tf_op jit(solution)/shard_map/ppermute | solution.py:213
  33.6 66.8 %collective-permute-start.1 = (f32[512,512]{1,0:T(8,128)}, f32[512,512]{1,0:T(8,128)S(1)}, u32[]{:S(2)}, u32[]{:S(2)}) collective-permute-start(f32[512,512]{1,0:T(8,128)} %get-tuple-element.112), channel_id=1, source_target_pairs={{1,0},{3,2},{5,4},{7,6},{9,8},{11,10},{13,12},{15,14},{17,16},{19,... | collective-permute-start | bytes 3145736 | tf_op jit(solution)/shard_map/ppermute | solution.py:237
